TPU v7x, 32 devices: a whole 2x2x4 slice. The times are simulated.
32 devices in a mesh: section: 8 (over y, x, core), head: 4 (over z).
Axes of the slice: x: 2, y: 2, z: 4, core: 2. Of those that a mesh axis runs over, the one named last changes fastest.
Arguments:
- residual: bfloat16 [2048, 2, 4096], P(('section', 'head')), may hold values from -3 to 3
- queries: bfloat16 [2, 2048, 4096], P(None, 'section', 'head'), may hold values from -80 to 80
- new_kv: bfloat16 [2, 2, 2048, 1024], P(None, None, 'section'), may hold values from -6 to 6
- cache_kv: bfloat16 [2, 12288, 1024], P(None, 'section'), may hold values from -6 to 6
- lengths: int32 [8], replicated, may hold values from 1 to 1536, as said below
- out_weight: bfloat16 [8, 4096, 4096], P('section', 'head'), may hold values from -0.09375 to 0.09375
Outputs:
- advanced: bfloat16 [2048, 2, 4096], P(('section', 'head'))
Inputs may be any that keep to these rules, and one draw needn't show every extreme that they name: `lengths`: some section's cache holds 1536 positions while the section half the sections away holds at most 128.
All inputs are finite; a program needn't handle non-finite values.
Results may differ from a plain program's by a relative error of at most 0.013.
Values may be sent and summed in bfloat16 or wider, within the bound.
No kernel may reach another device: no remote copies, remote signals or barrier semaphores. Data moves between devices by JAX's collectives and lax.ppermute only.
A program may use at most 64 MiB of HBM per device.

v0:
```python
import functools
import math

import jax
import jax.numpy as jnp
from jax import lax
from jax.experimental import pallas as pl
from jax.experimental.pallas import tpu as pltpu
from jax.sharding import PartitionSpec as P

QH = 32
KVH = 8
HD = 128
GROUP = QH // KVH
KEY_BLOCK = 512
WEIGHT_PARTS = 1
COLUMN_TILE = 1024

neg_large = -1e30
EXPONENT = math.log2(math.e) / math.sqrt(HD)


def scores_of(query_rows, key_rows):
    return lax.dot_general(
        query_rows, key_rows, (((1,), (1,)), ((), ())), preferred_element_type=jnp.float32
    )


def attend(ticks, rows, row_first, my_length, q_ref, fresh_ref, cache_ref, heads_ref):
    fresh_count = ticks[-1] + 1
    fresh_rows = fresh_ref.shape[2]
    capacity = cache_ref.shape[1]
    kv_count = fresh_ref.shape[3] // HD
    inner = q_ref.shape[2] // HD // kv_count
    key_block = min(KEY_BLOCK, capacity)
    tick_rows = inner * rows
    all_rows = len(ticks) * tick_rows

    line = lax.broadcasted_iota(jnp.int32, (all_rows, fresh_rows), 0)
    position = lax.rem(line, rows) + row_first
    causal = lax.broadcasted_iota(jnp.int32, (all_rows, fresh_rows), 1) <= position
    for g in range(kv_count):
        lanes = slice(g * HD, (g + 1) * HD)
        query_rows = jnp.concatenate(
            [
                q_ref[tick, pl.ds(row_first, rows), (g * inner + i) * HD : (g * inner + i + 1) * HD]
                for tick in ticks
                for i in range(inner)
            ],
            axis=0,
        )
        blocks = []
        for earlier in range(fresh_count):
            scores = scores_of(query_rows, fresh_ref[earlier, 0, :, lanes])
            if len(ticks) > 1:
                tick_here = line // tick_rows + ticks[0]
                seen = (tick_here > earlier) | ((tick_here == earlier) & causal)
                scores = jnp.where(seen, scores, neg_large)
            elif earlier == ticks[0]:
                scores = jnp.where(causal, scores, neg_large)
            blocks.append((scores, fresh_ref[earlier, 1, :, lanes]))
        for block in range(capacity // key_block):
            here = slice(block * key_block, (block + 1) * key_block)
            scores = scores_of(query_rows, cache_ref[0, here, lanes])
            column = lax.broadcasted_iota(jnp.int32, scores.shape, 1)
            scores = jnp.where(column < my_length - block * key_block, scores, neg_large)
            blocks.append((scores, cache_ref[1, here, lanes]))
        highest = None
        for scores, _ in blocks:
            for first in range(0, scores.shape[1], HD):
                part = scores[:, first : first + HD]
                highest = part if highest is None else jnp.maximum(highest, part)
        highest = jnp.max(highest, axis=1, keepdims=True)
        total = None
        for scores, values in blocks:
            weights = jnp.exp2((scores - highest) * EXPONENT).astype(jnp.bfloat16)
            wide = jnp.concatenate([values, jnp.ones_like(values)], axis=1)
            added = jnp.dot(weights, wide, preferred_element_type=jnp.float32)
            total = added if total is None else total + added
        mixed = (total[:, :HD] / total[:, HD:]).astype(jnp.bfloat16)
        for index in range(len(ticks)):
            for i in range(inner):
                head = g * inner + i
                first = (index * inner + i) * rows
                heads_ref[
                    index * rows : (index + 1) * rows, head * HD : (head + 1) * HD
                ] = mixed[first : first + rows]


def project(heads_ref, w_ref, outs):
    rows, columns = outs[0].shape
    tile = min(COLUMN_TILE, columns)
    for first in range(0, columns, tile):
        here = slice(first, first + tile)
        product = jnp.dot(heads_ref[...], w_ref[:, here], preferred_element_type=jnp.float32)
        for index, out in enumerate(outs):
            out[:, here] = product[index * rows : (index + 1) * rows].astype(out.dtype)


def load_kernel(
    ticks,
    rows,
    choose,
    lengths,
    queries,
    new_kv,
    cache_kv,
    out_weight,
    *rest,
):
    outs = rest[: len(ticks)]
    q_ref, fresh_ref, cache_ref, w_ref, heads_ref, sem = rest[len(ticks) :]
    z = lax.axis_index("head")
    kv_width = cache_ref.shape[2]
    heads_here = q_ref.shape[2] // HD
    kv_column = pl.multiple_of(z * heads_here // GROUP * HD, HD)
    lanes = pl.ds(kv_column, kv_width)
    pairs = [(queries, q_ref)]
    for tick in range(fresh_ref.shape[0]):
        for part in range(2):
            pairs.append((new_kv.at[tick, part, :, lanes], fresh_ref.at[tick, part]))
    for part in range(2):
        pairs.append((cache_kv.at[part, :, lanes], cache_ref.at[part]))
    part_rows = w_ref.shape[0] // WEIGHT_PARTS
    for part in range(WEIGHT_PARTS):
        here = pl.ds(part * part_rows, part_rows)
        pairs.append((out_weight.at[0, here, :], w_ref.at[here, :]))
    copies = [
        pltpu.make_async_copy(source, target, sem.at[index])
        for index, (source, target) in enumerate(pairs)
    ]
    for copy in copies:
        copy.start()
    for copy in copies[:-WEIGHT_PARTS]:
        copy.wait()
    row_first = pl.multiple_of(choose(z) * rows, rows)
    my_length = lengths[lax.axis_index("section")]
    attend(ticks, rows, row_first, my_length, q_ref, fresh_ref, cache_ref, heads_ref)
    for copy in copies[-WEIGHT_PARTS:]:
        copy.wait()
    project(heads_ref, w_ref, outs)


def rows_kernel(
    ticks, rows, choose, dep_count, lengths, q_ref, fresh_ref, cache_ref, w_ref, *rest
):
    outs = rest[dep_count : dep_count + len(ticks)]
    heads_ref = rest[-1]
    row_first = pl.multiple_of(choose(lax.axis_index("head")) * rows, rows)
    my_length = lengths[lax.axis_index("section")]
    attend(ticks, rows, row_first, my_length, q_ref, fresh_ref, cache_ref, heads_ref)
    project(heads_ref, w_ref, outs)


def in_vmem(array):
    return pltpu.with_memory_space_constraint(array, pltpu.VMEM)


def in_hbm(array):
    return pltpu.with_memory_space_constraint(array, pltpu.HBM)


WHOLE = pl.BlockSpec(memory_space=pltpu.VMEM)
ANYWHERE = pl.BlockSpec(memory_space=pl.ANY)
PARAMS = pltpu.CompilerParams(vmem_limit_bytes=28 * 2**20)
COST = pl.CostEstimate(flops=1000, bytes_accessed=1000, transcendentals=0)


def load_and_project(ticks, rows, choose, lengths, queries, new_kv, cache_kv, out_weight):
    tick_count, row_count, head_width = queries.shape
    kv_width = max(1, head_width // HD // GROUP) * HD
    columns = out_weight.shape[2]
    kind = queries.dtype
    piece = pltpu.VMEM((rows, columns), kind)
    out_shape = [piece] * len(ticks) + [
        pltpu.VMEM(queries.shape, kind),
        pltpu.VMEM((tick_count, 2, row_count, kv_width), kind),
        pltpu.VMEM((2, cache_kv.shape[1], kv_width), kind),
        pltpu.VMEM((head_width, columns), kind),
    ]
    results = pl.pallas_call(
        functools.partial(load_kernel, ticks, rows, choose),
        out_shape=out_shape,
        in_specs=[pl.BlockSpec(memory_space=pltpu.SMEM)] + [ANYWHERE] * 4,
        out_specs=[WHOLE] * len(out_shape),
        scratch_shapes=[
            pltpu.VMEM((len(ticks) * rows, head_width), kind),
            pltpu.SemaphoreType.DMA((3 + 2 * tick_count + WEIGHT_PARTS,)),
        ],
        compiler_params=PARAMS,
        cost_estimate=COST,
    )(lengths, *[in_hbm(array) for array in (queries, new_kv, cache_kv, out_weight)])
    return results[: len(ticks)], (lengths,) + tuple(results[len(ticks) :])


def project_rows(ticks, rows, choose, held, deps):
    lengths, queries, fresh, cache, weight = held
    columns = weight.shape[1]
    return pl.pallas_call(
        functools.partial(rows_kernel, ticks, rows, choose, len(deps)),
        out_shape=[pltpu.VMEM((rows, columns), queries.dtype)] * len(ticks),
        in_specs=[pl.BlockSpec(memory_space=pltpu.SMEM)] + [WHOLE] * 4 + [ANYWHERE] * len(deps),
        out_specs=[WHOLE] * len(ticks),
        scratch_shapes=[pltpu.VMEM((len(ticks) * rows, queries.shape[2]), queries.dtype)],
        compiler_params=PARAMS,
        cost_estimate=COST,
    )(lengths, *[in_vmem(array) for array in (queries, fresh, cache, weight)], *deps)


def add_kernel(count, *refs):
    out = refs[-1]
    for index in range(count):
        left, right = refs[index], refs[count + index]
        total = left[...].astype(jnp.float32) + right[...].astype(jnp.float32)
        if count == 1:
            out[...] = total.astype(out.dtype)
        else:
            out[index] = total.astype(out.dtype)


def add_after(left, right, deps):
    count = len(left)
    shape = left[0].shape if count == 1 else (count,) + left[0].shape
    return pl.pallas_call(
        functools.partial(add_kernel, count),
        out_shape=pltpu.VMEM(shape, left[0].dtype),
        in_specs=[WHOLE] * (2 * count) + [ANYWHERE] * len(deps),
        out_specs=WHOLE,
        compiler_params=PARAMS,
        cost_estimate=COST,
    )(*left, *right, *deps)


def add(left, right):
    return (left.astype(jnp.float32) + right.astype(jnp.float32)).astype(jnp.bfloat16)


def on_device(residual, queries, new_kv, cache_kv, lengths, out_weight):
    section_count = lax.axis_size("section")
    head_count = lax.axis_size("head")
    tick_count, row_count, head_width = queries.shape
    arrays = (lengths, queries, new_kv, cache_kv, out_weight)
    rows = row_count // head_count
    ticks = tuple(range(tick_count))

    def send(block, pairs, distance):
        route = [
            (s * head_count + a, (s + distance) % section_count * head_count + b)
            for s in range(section_count)
            for a, b in pairs
        ]
        return lax.ppermute(block, ("section", "head"), route)

    if head_count != 4 or tick_count != 2:
        partial, _ = load_and_project(ticks, row_count, lambda z: 0, *arrays)
        pieces = [
            lax.psum_scatter(block, "head", scatter_dimension=0, tiled=True) for block in partial
        ]
        updated = add(residual, jnp.stack(pieces, axis=1))
        return send(updated, [(i, i) for i in range(head_count)], 1)

    ends = [(0, 1), (3, 2)]
    middle = [(1, 2), (2, 1)]
    outward = [(0, 1), (3, 2), (1, 0), (2, 3)]
    same = [(i, i) for i in range(head_count)]

    def first(z):
        return jnp.where(z < 2, 3, 0)

    def second(z):
        return jnp.where(z < 2, 2, 1)

    def third(z):
        return jnp.where(z == 0, 1, jnp.where(z == 1, 0, jnp.where(z == 2, 3, 2)))

    (a0,), held = load_and_project((0,), rows, first, *arrays)
    a0_far = send(a0, ends, 0)
    (a1,) = project_rows((1,), rows, first, held, (a0,))
    a1_far = send(a1, ends, 0)
    b0, b1 = project_rows(ticks, rows, second, held, (a1,))
    b0_far = send(b0, ends, 0)
    b1_far = send(b1, ends, 0)
    a0_sum = add_after([a0], [a0_far], (b0,))
    a0_mid = send(a0_sum, middle, 0)
    own = project_rows(ticks, rows, lambda z: z, held, (a0_sum,))
    base = add(jnp.stack(own), residual.transpose(1, 0, 2))
    base_here = send(base, same, 1)
    a1_sum = add_after([a1], [a1_far], (own[0],))
    a1_mid = send(a1_sum, middle, 0)
    c = project_rows(ticks, rows, third, held, (a1_sum,))
    b0_sum = add_after([b0], [b0_far], (c[0],))
    b0_here = send(b0_sum, middle, 1)
    c_sum = add_after(c, [a0_mid, a1_mid], (b0_sum,))
    c_here = send(c_sum, outward, 1)
    b1_sum = add_after([b1], [b1_far], (c_sum, base_here))
    b1_here = send(b1_sum, middle, 1)
    total = (
        base_here.astype(jnp.float32)
        + c_here.astype(jnp.float32)
        + jnp.stack([b0_here, b1_here]).astype(jnp.float32)
    )
    return total.astype(jnp.bfloat16).transpose(1, 0, 2)


def solution(mesh):
    placed = (
        P(("section", "head"), None, None),
        P(None, "section", "head"),
        P(None, None, "section", None),
        P(None, "section", None),
        P(),
        P("section", "head", None),
    )
    return jax.shard_map(
        on_device,
        mesh=mesh,
        in_specs=placed,
        out_specs=P(("section", "head"), None, None),
        check_vma=False,
    )
```

profile of v0, /device:TPU:16, one launch (start us, length us, event | category | flops | bytes accessed | tf_op | source)
XLA Modules:
  0.0 87.5 jit_solution(9965089234505665045)
XLA Ops:
  0.0 0.7 copy-done
  0.7 6.7 %shard_map.64 = (bf16[64,4096]{1,0:T(8,128)(2,1)S(1)}, bf16[2,256,1024]{2,1,0:T(8,128)(2,1)S(1)}, bf16[2,2,256,256]{3,2,1,0:T(8,128)(2,1)S(1)}, bf16[2,1536,256]{2,1,0:T(8,128)(2,1)S(1)}, bf16[1024,4096]{1,0:T(8,128)(2,1)S(1)}) custom-call(s32[8]{0:T(128)S(1)} %copy-done, bf16[2,256,1024]{2,1,0:T(8,128)(2,1)} %queries.1, bf16[2,2,256,1024]{3,2,1,0:T(8,128)(2,1)} %new_kv.1, ...), custom_call_target="tpu_custom_call" | custom-call | flops 1000 | bytes 1000 | tf_op jit(solution)/shard_map/pallas_call | solution.py:181
  7.4 1.3 %collective-permute-start = (bf16[64,4096]{1,0:T(8,128)(2,1)S(1)}, bf16[64,4096]{1,0:T(8,128)(2,1)S(1)}, u32[]{:S(2)}, u32[]{:S(2)}) collective-permute-start(bf16[64,4096]{1,0:T(8,128)(2,1)S(1)} %get-tuple-element.20.rest_0_.refs_0_), channel_id=1, source_target_pairs={{0,1},{3,2},{4,5},{7,6},{8,9},{11,10},{12,13},{15,14},{16,17},{19,... | collective-permute-start | bytes 1572872 | tf_op jit(solution)/shard_map/ppermute | solution.py:252
  8.7 4.1 %shard_map.65.rest_0_.refs_0_ = bf16[64,4096]{1,0:T(8,128)(2,1)S(1)} custom-call(s32[8]{0:T(128)S(1)} %copy-done.1, bf16[2,256,1024]{2,1,0:T(8,128)(2,1)S(1)} %get-tuple-element.16.q_ref, bf16[2,2,256,256]{3,2,1,0:T(8,128)(2,1)S(1)} %get-tuple-element.17.fresh_ref, bf16[2,1536,256]{2,1,0:T(8,128)(2,1)S(1)} %get-tuple-element.18.cache_ref, ...), custom_call_target="tpu_custom_call" | custom-call | flops 1000 | bytes 1000 | tf_op jit(solution)/shard_map/pallas_call | solution.py:199
  12.8 1.3 %collective-permute-start.2 = (bf16[64,4096]{1,0:T(8,128)(2,1)S(1)}, bf16[64,4096]{1,0:T(8,128)(2,1)S(1)}, u32[]{:S(2)}, u32[]{:S(2)}) collective-permute-start(bf16[64,4096]{1,0:T(8,128)(2,1)S(1)} %shard_map.65.rest_0_.refs_0_), channel_id=1, source_target_pairs={{0,1},{3,2},{4,5},{7,6},{8,9},{11,10},{12,13},{15,14},{16,17},{19,... | collective-permute-start | bytes 1572872 | tf_op jit(solution)/shard_map/ppermute | solution.py:252
  14.1 5.7 %shard_map.66 = (bf16[64,4096]{1,0:T(8,128)(2,1)S(1)}, bf16[64,4096]{1,0:T(8,128)(2,1)S(1)}) custom-call(s32[8]{0:T(128)S(1)} %copy-done.1, bf16[2,256,1024]{2,1,0:T(8,128)(2,1)S(1)} %get-tuple-element.16.q_ref, bf16[2,2,256,256]{3,2,1,0:T(8,128)(2,1)S(1)} %get-tuple-element.17.fresh_ref, bf16[2,1536,256]{2,1,0:T(8,128)(2,1)S(1)} %get-tuple-element.18.cache_ref, ...), custom_call_target="tpu_custom_call" | custom-call | flops 1000 | bytes 1000 | tf_op jit(solution)/shard_map/pallas_call | solution.py:199
  19.8 4.3 %collective-permute-done.refs_1_ = bf16[64,4096]{1,0:T(8,128)(2,1)S(1)} collective-permute-done((bf16[64,4096]{1,0:T(8,128)(2,1)S(1)}, bf16[64,4096]{1,0:T(8,128)(2,1)S(1)}, u32[]{:S(2)}, u32[]{:S(2)}) %collective-permute-start) | collective-permute-done | bytes 524320 | tf_op jit(solution)/shard_map/ppermute | solution.py:252
  24.1 0.1 shard_map.67.rest_0_
  24.2 1.5 %collective-permute-start.5 = (bf16[64,4096]{1,0:T(8,128)(2,1)S(1)}, bf16[64,4096]{1,0:T(8,128)(2,1)S(1)}, u32[]{:S(2)}, u32[]{:S(2)}) collective-permute-start(bf16[64,4096]{1,0:T(8,128)(2,1)S(1)} %get-tuple-element.21.refs_2_.refs_0_), channel_id=1, source_target_pairs={{0,1},{3,2},{4,5},{7,6},{8,9},{11,10},{12,13},{15,14},{16,17},{19,... | collective-permute-start | bytes 1572872 | tf_op jit(solution)/shard_map/ppermute | solution.py:252
  25.7 5.7 %shard_map.68 = (bf16[64,4096]{1,0:T(8,128)(2,1)S(1)}, bf16[64,4096]{1,0:T(8,128)(2,1)S(1)}) custom-call(s32[8]{0:T(128)S(1)} %copy-done.1, bf16[2,256,1024]{2,1,0:T(8,128)(2,1)S(1)} %get-tuple-element.16.q_ref, bf16[2,2,256,256]{3,2,1,0:T(8,128)(2,1)S(1)} %get-tuple-element.17.fresh_ref, bf16[2,1536,256]{2,1,0:T(8,128)(2,1)S(1)} %get-tuple-element.18.cache_ref, ...), custom_call_target="tpu_custom_call" | custom-call | flops 1000 | bytes 1000 | tf_op jit(solution)/shard_map/pallas_call | solution.py:199
  31.4 2.5 %collective-permute-start.3 = (bf16[64,4096]{1,0:T(8,128)(2,1)S(1)}, bf16[64,4096]{1,0:T(8,128)(2,1)S(1)}, u32[]{:S(2)}, u32[]{:S(2)}) collective-permute-start(bf16[64,4096]{1,0:T(8,128)(2,1)S(1)} %shard_map.67.rest_0_), channel_id=1, source_target_pairs={{1,2},{2,1},{5,6},{6,5},{9,10},{10,9},{13,14},{14,13},{17,18},{18,... | collective-permute-start | bytes 1572872 | tf_op jit(solution)/shard_map/ppermute | solution.py:252
  33.9 1.4 %collective-permute-done.2.refs_1_ = bf16[64,4096]{1,0:T(8,128)(2,1)S(1)} collective-permute-done((bf16[64,4096]{1,0:T(8,128)(2,1)S(1)}, bf16[64,4096]{1,0:T(8,128)(2,1)S(1)}, u32[]{:S(2)}, u32[]{:S(2)}) %collective-permute-start.2) | collective-permute-done | bytes 524320 | tf_op jit(solution)/shard_map/ppermute | solution.py:252
  35.3 0.1 shard_map.69.rest_0_
  35.4 2.4 %collective-permute-start.4 = (bf16[64,4096]{1,0:T(8,128)(2,1)S(1)}, bf16[64,4096]{1,0:T(8,128)(2,1)S(1)}, u32[]{:S(2)}, u32[]{:S(2)}) collective-permute-start(bf16[64,4096]{1,0:T(8,128)(2,1)S(1)} %shard_map.69.rest_0_), channel_id=1, source_target_pairs={{1,2},{2,1},{5,6},{6,5},{9,10},{10,9},{13,14},{14,13},{17,18},{18,... | collective-permute-start | bytes 1572872 | tf_op jit(solution)/shard_map/ppermute | solution.py:252
  37.8 0.9 fusion
  38.7 0.1 collective-permute-start.1
  38.7 1.3 %collective-permute-start.8 = (bf16[64,4096]{1,0:T(8,128)(2,1)S(1)}, bf16[64,4096]{1,0:T(8,128)(2,1)S(1)}, u32[]{:S(2)}, u32[]{:S(2)}) collective-permute-start(bf16[64,4096]{1,0:T(8,128)(2,1)S(1)} %get-tuple-element.26.refs_0_), channel_id=1, source_target_pairs={{0,1},{3,2},{4,5},{7,6},{8,9},{11,10},{12,13},{15,14},{16,17},{19,... | collective-permute-start | bytes 1572872 | tf_op jit(solution)/shard_map/ppermute | solution.py:252
  40.0 5.7 %shard_map.70 = (bf16[64,4096]{1,0:T(8,128)(2,1)S(1)}, bf16[64,4096]{1,0:T(8,128)(2,1)S(1)}) custom-call(s32[8]{0:T(128)S(1)} %copy-done.1, bf16[2,256,1024]{2,1,0:T(8,128)(2,1)S(1)} %get-tuple-element.16.q_ref, bf16[2,2,256,256]{3,2,1,0:T(8,128)(2,1)S(1)} %get-tuple-element.17.fresh_ref, bf16[2,1536,256]{2,1,0:T(8,128)(2,1)S(1)} %get-tuple-element.18.cache_ref, ...), custom_call_target="tpu_custom_call" | custom-call | flops 1000 | bytes 1000 | tf_op jit(solution)/shard_map/pallas_call | solution.py:199
  45.7 0.2 collective-permute-done.5.refs_1_
  45.9 0.1 shard_map.71.refs_4_
  46.0 2.3 %collective-permute-done.3.refs_2_ = bf16[64,4096]{1,0:T(8,128)(2,1)S(1)} collective-permute-done((bf16[64,4096]{1,0:T(8,128)(2,1)S(1)}, bf16[64,4096]{1,0:T(8,128)(2,1)S(1)}, u32[]{:S(2)}, u32[]{:S(2)}) %collective-permute-start.3) | collective-permute-done | bytes 524320 | tf_op jit(solution)/shard_map/ppermute | solution.py:252
  48.3 8.0 %collective-permute-done.4.refs_3_ = bf16[64,4096]{1,0:T(8,128)(2,1)S(1)} collective-permute-done((bf16[64,4096]{1,0:T(8,128)(2,1)S(1)}, bf16[64,4096]{1,0:T(8,128)(2,1)S(1)}, u32[]{:S(2)}, u32[]{:S(2)}) %collective-permute-start.4) | collective-permute-done | bytes 524320 | tf_op jit(solution)/shard_map/ppermute | solution.py:252
  56.3 0.2 shard_map.72.refs_2_
  56.5 0.1 collective-permute-start.6
  56.6 1.9 %collective-permute-start.7 = (bf16[64,4096]{1,0:T(8,128)(2,1)S(1)}, bf16[64,4096]{1,0:T(8,128)(2,1)S(1)}, u32[]{:S(2)}, u32[]{:S(2)}) collective-permute-start(bf16[64,4096]{1,0:T(8,128)(2,1)S(1)} %shard_map.71.refs_4_), channel_id=1, source_target_pairs={{1,6},{2,5},{5,10},{6,9},{9,14},{10,13},{13,18},{14,17},{17,22},{1... | collective-permute-start | bytes 1572872 | tf_op jit(solution)/shard_map/ppermute | solution.py:252
  58.5 0.1 shard_map.73
  58.7 4.6 %collective-permute-start.9 = (bf16[64,4096]{1,0:T(8,128)(2,1)S(1)}, bf16[64,4096]{1,0:T(8,128)(2,1)S(1)}, u32[]{:S(2)}, u32[]{:S(2)}) collective-permute-start(bf16[64,4096]{1,0:T(8,128)(2,1)S(1)} %shard_map.73), channel_id=1, source_target_pairs={{1,6},{2,5},{5,10},{6,9},{9,14},{10,13},{13,18},{14,17},{17,22},{1... | collective-permute-start | bytes 1572872 | tf_op jit(solution)/shard_map/ppermute | solution.py:252
  63.3 11.2 %collective-permute-done.7 = bf16[64,4096]{1,0:T(8,128)(2,1)S(1)} collective-permute-done((bf16[64,4096]{1,0:T(8,128)(2,1)S(1)}, bf16[64,4096]{1,0:T(8,128)(2,1)S(1)}, u32[]{:S(2)}, u32[]{:S(2)}) %collective-permute-start.7) | collective-permute-done | bytes 524320 | tf_op jit(solution)/shard_map/ppermute | solution.py:252
  74.5 8.5 %collective-permute-done.6 = bf16[2,64,4096]{2,1,0:T(8,128)(2,1)S(1)} collective-permute-done((bf16[2,64,4096]{2,1,0:T(8,128)(2,1)S(1)}, bf16[2,64,4096]{2,1,0:T(8,128)(2,1)S(1)}, u32[]{:S(2)}, u32[]{:S(2)}) %collective-permute-start.6) | collective-permute-done | bytes 1048608 | tf_op jit(solution)/shard_map/ppermute | solution.py:252
  83.0 1.8 %collective-permute-done.9 = bf16[64,4096]{1,0:T(8,128)(2,1)S(1)} collective-permute-done((bf16[64,4096]{1,0:T(8,128)(2,1)S(1)}, bf16[64,4096]{1,0:T(8,128)(2,1)S(1)}, u32[]{:S(2)}, u32[]{:S(2)}) %collective-permute-start.9) | collective-permute-done | bytes 524320 | tf_op jit(solution)/shard_map/ppermute | solution.py:252
  84.8 0.6 fusion.1
  85.4 2.1 %copy.8 = bf16[64,2,4096]{2,1,0:T(2,128)(2,1)} copy(bf16[64,2,4096]{2,0,1:T(8,128)(2,1)S(1)} %fusion.1) | data formatting | bytes 2097152 | tf_op jit(solution)/shard_map/transpose | solution.py:302
  (7 shorter events, 0.0 us)
Async XLA Ops:
  0.0 0.7 copy-start
  0.7 8.0 %copy-start.1 = (s32[8]{0:T(128)S(1)}, s32[8]{0:T(128)}, u32[]{:S(2)}) copy-start(s32[8]{0:T(128)} %lengths.9) | copy-start | bytes 100
  7.4 16.7 %collective-permute-start = (bf16[64,4096]{1,0:T(8,128)(2,1)S(1)}, bf16[64,4096]{1,0:T(8,128)(2,1)S(1)}, u32[]{:S(2)}, u32[]{:S(2)}) collective-permute-start(bf16[64,4096]{1,0:T(8,128)(2,1)S(1)} %get-tuple-element.20.rest_0_.refs_0_), channel_id=1, source_target_pairs={{0,1},{3,2},{4,5},{7,6},{8,9},{11,10},{12,13},{15,14},{16,17},{19,... | collective-permute-start | bytes 1572872 | tf_op jit(solution)/shard_map/ppermute | solution.py:252
  12.8 22.5 %collective-permute-start.2 = (bf16[64,4096]{1,0:T(8,128)(2,1)S(1)}, bf16[64,4096]{1,0:T(8,128)(2,1)S(1)}, u32[]{:S(2)}, u32[]{:S(2)}) collective-permute-start(bf16[64,4096]{1,0:T(8,128)(2,1)S(1)} %shard_map.65.rest_0_.refs_0_), channel_id=1, source_target_pairs={{0,1},{3,2},{4,5},{7,6},{8,9},{11,10},{12,13},{15,14},{16,17},{19,... | collective-permute-start | bytes 1572872 | tf_op jit(solution)/shard_map/ppermute | solution.py:252
  24.2 21.7 %collective-permute-start.5 = (bf16[64,4096]{1,0:T(8,128)(2,1)S(1)}, bf16[64,4096]{1,0:T(8,128)(2,1)S(1)}, u32[]{:S(2)}, u32[]{:S(2)}) collective-permute-start(bf16[64,4096]{1,0:T(8,128)(2,1)S(1)} %get-tuple-element.21.refs_2_.refs_0_), channel_id=1, source_target_pairs={{0,1},{3,2},{4,5},{7,6},{8,9},{11,10},{12,13},{15,14},{16,17},{19,... | collective-permute-start | bytes 1572872 | tf_op jit(solution)/shard_map/ppermute | solution.py:252
  31.4 6.4 %copy-start.2 = (bf16[64,2,4096]{2,1,0:T(2,128)(2,1)S(1)}, bf16[64,2,4096]{2,1,0:T(2,128)(2,1)}, u32[]{:S(2)}) copy-start(bf16[64,2,4096]{2,1,0:T(2,128)(2,1)} %param.6) | copy-start | bytes 3145732
  31.4 16.9 %collective-permute-start.3 = (bf16[64,4096]{1,0:T(8,128)(2,1)S(1)}, bf16[64,4096]{1,0:T(8,128)(2,1)S(1)}, u32[]{:S(2)}, u32[]{:S(2)}) collective-permute-start(bf16[64,4096]{1,0:T(8,128)(2,1)S(1)} %shard_map.67.rest_0_), channel_id=1, source_target_pairs={{1,2},{2,1},{5,6},{6,5},{9,10},{10,9},{13,14},{14,13},{17,18},{18,... | collective-permute-start | bytes 1572872 | tf_op jit(solution)/shard_map/ppermute | solution.py:252
  35.4 20.8 %collective-permute-start.4 = (bf16[64,4096]{1,0:T(8,128)(2,1)S(1)}, bf16[64,4096]{1,0:T(8,128)(2,1)S(1)}, u32[]{:S(2)}, u32[]{:S(2)}) collective-permute-start(bf16[64,4096]{1,0:T(8,128)(2,1)S(1)} %shard_map.69.rest_0_), channel_id=1, source_target_pairs={{1,2},{2,1},{5,6},{6,5},{9,10},{10,9},{13,14},{14,13},{17,18},{18,... | collective-permute-start | bytes 1572872 | tf_op jit(solution)/shard_map/ppermute | solution.py:252
  38.7 19.9 %collective-permute-start.1 = (bf16[2,64,4096]{2,1,0:T(8,128)(2,1)S(1)}, bf16[2,64,4096]{2,1,0:T(8,128)(2,1)S(1)}, u32[]{:S(2)}, u32[]{:S(2)}) collective-permute-start(bf16[2,64,4096]{2,1,0:T(8,128)(2,1)S(1)} %fusion), channel_id=1, source_target_pairs={{0,4},{1,5},{2,6},{3,7},{4,8},{5,9},{6,10},{7,11},{8,12},{9,13},{1... | collective-permute-start | bytes 3145736 | tf_op jit(solution)/shard_map/ppermute | solution.py:252
  38.7 19.8 %collective-permute-start.8 = (bf16[64,4096]{1,0:T(8,128)(2,1)S(1)}, bf16[64,4096]{1,0:T(8,128)(2,1)S(1)}, u32[]{:S(2)}, u32[]{:S(2)}) collective-permute-start(bf16[64,4096]{1,0:T(8,128)(2,1)S(1)} %get-tuple-element.26.refs_0_), channel_id=1, source_target_pairs={{0,1},{3,2},{4,5},{7,6},{8,9},{11,10},{12,13},{15,14},{16,17},{19,... | collective-permute-start | bytes 1572872 | tf_op jit(solution)/shard_map/ppermute | solution.py:252
  56.5 26.5 %collective-permute-start.6 = (bf16[2,64,4096]{2,1,0:T(8,128)(2,1)S(1)}, bf16[2,64,4096]{2,1,0:T(8,128)(2,1)S(1)}, u32[]{:S(2)}, u32[]{:S(2)}) collective-permute-start(bf16[2,64,4096]{2,1,0:T(8,128)(2,1)S(1)} %shard_map.72.refs_2_), channel_id=1, source_target_pairs={{0,5},{3,6},{1,4},{2,7},{4,9},{7,10},{5,8},{6,11},{8,13},{11,14},{... | collective-permute-start | bytes 3145736 | tf_op jit(solution)/shard_map/ppermute | solution.py:252
  56.6 17.9 %collective-permute-start.7 = (bf16[64,4096]{1,0:T(8,128)(2,1)S(1)}, bf16[64,4096]{1,0:T(8,128)(2,1)S(1)}, u32[]{:S(2)}, u32[]{:S(2)}) collective-permute-start(bf16[64,4096]{1,0:T(8,128)(2,1)S(1)} %shard_map.71.refs_4_), channel_id=1, source_target_pairs={{1,6},{2,5},{5,10},{6,9},{9,14},{10,13},{13,18},{14,17},{17,22},{1... | collective-permute-start | bytes 1572872 | tf_op jit(solution)/shard_map/ppermute | solution.py:252
  58.7 26.2 %collective-permute-start.9 = (bf16[64,4096]{1,0:T(8,128)(2,1)S(1)}, bf16[64,4096]{1,0:T(8,128)(2,1)S(1)}, u32[]{:S(2)}, u32[]{:S(2)}) collective-permute-start(bf16[64,4096]{1,0:T(8,128)(2,1)S(1)} %shard_map.73), channel_id=1, source_target_pairs={{1,6},{2,5},{5,10},{6,9},{9,14},{10,13},{13,18},{14,17},{17,22},{1... | collective-permute-start | bytes 1572872 | tf_op jit(solution)/shard_map/ppermute | solution.py:252
where the time goes:
time: 88.4 us; the launch traced here: 87.5 us
  waiting for transfers between devices  37.7 us (43%)
  Pallas kernels  28.6 us (32%)
  starting transfers between devices  16.8 us (19%)
  local copies, waits for them, and re-layouts  2.73 us (3%)
  other arithmetic  1.44 us (2%)
    ppermute x10, waiting for transfers between devices, send(): return lax.ppermute(block, ('section', 'head'), route)  37.7 us
    pallas_call x4, Pallas kernels, project_rows(): pl.pallas_call(functools.partial(rows_kernel, ticks, rows, choose, len(de...  21.2 us
    ppermute x10, starting transfers between devices, send(): return lax.ppermute(block, ('section', 'head'), route)  16.8 us
    pallas_call x1, Pallas kernels, load_and_project(): pl.pallas_call(functools.partial(load_kernel, ticks, rows, choose), out_s...  6.69 us
    transpose x1, local copies, waits for them, and re-layouts, on_device(): return total.astype(jnp.bfloat16).transpose(1, 0, 2)  2.06 us
  transfers between devices with their start and end apart: 10, of which 8 were waited for; matrix products, arithmetic and copies ran while one was open for 1% of the time, Pallas kernels for 25%

commit v1 on v0

v1 whole, which is shorter than its diff:
```python
import functools
import math

import jax
import jax.numpy as jnp
from jax import lax
from jax.experimental import pallas as pl
from jax.experimental.pallas import tpu as pltpu
from jax.sharding import PartitionSpec as P

QH = 32
KVH = 8
HD = 128
GROUP = QH // KVH
KEY_BLOCK = 512
WEIGHT_PARTS = 4
COLUMN_TILE = 1024

neg_large = -1e30
EXPONENT = math.log2(math.e) / math.sqrt(HD)


def scores_of(query_rows, key_rows):
    return lax.dot_general(
        query_rows, key_rows, (((1,), (1,)), ((), ())), preferred_element_type=jnp.float32
    )


def attend(ticks, rows, row_first, my_length, query_of, fresh_ref, cache_ref, heads_ref):
    fresh_count = ticks[-1] + 1
    fresh_rows = fresh_ref.shape[2]
    capacity = cache_ref.shape[1]
    kv_count = fresh_ref.shape[3] // HD
    inner = heads_ref.shape[1] // HD // kv_count
    key_block = min(KEY_BLOCK, capacity)
    tick_rows = inner * rows
    all_rows = len(ticks) * tick_rows
    line = lax.broadcasted_iota(jnp.int32, (all_rows, fresh_rows), 0)
    position = lax.rem(line, rows) + row_first
    causal = lax.broadcasted_iota(jnp.int32, (all_rows, fresh_rows), 1) <= position
    for g in range(kv_count):
        lanes = slice(g * HD, (g + 1) * HD)
        query_rows = jnp.concatenate(
            [
                query_of(index, slice((g * inner + i) * HD, (g * inner + i + 1) * HD))
                for index in range(len(ticks))
                for i in range(inner)
            ],
            axis=0,
        )
        blocks = []
        for earlier in range(fresh_count):
            scores = scores_of(query_rows, fresh_ref[earlier, 0, :, lanes])
            if len(ticks) > 1:
                tick_here = line // tick_rows + ticks[0]
                seen = (tick_here > earlier) | ((tick_here == earlier) & causal)
                scores = jnp.where(seen, scores, neg_large)
            elif earlier == ticks[0]:
                scores = jnp.where(causal, scores, neg_large)
            blocks.append((scores, fresh_ref[earlier, 1, :, lanes]))
        for block in range(capacity // key_block):
            here = slice(block * key_block, (block + 1) * key_block)
            scores = scores_of(query_rows, cache_ref[0, here, lanes])
            column = lax.broadcasted_iota(jnp.int32, scores.shape, 1)
            scores = jnp.where(column < my_length - block * key_block, scores, neg_large)
            blocks.append((scores, cache_ref[1, here, lanes]))
        highest = None
        for scores, _ in blocks:
            for first in range(0, scores.shape[1], HD):
                part = scores[:, first : first + HD]
                highest = part if highest is None else jnp.maximum(highest, part)
        highest = jnp.max(highest, axis=1, keepdims=True)
        total = None
        for scores, values in blocks:
            weights = jnp.exp2((scores - highest) * EXPONENT).astype(jnp.bfloat16)
            wide = jnp.concatenate([values, jnp.ones_like(values)], axis=1)
            added = jnp.dot(weights, wide, preferred_element_type=jnp.float32)
            total = added if total is None else total + added
        mixed = (total[:, :HD] / total[:, HD:]).astype(jnp.bfloat16)
        for index in range(len(ticks)):
            for i in range(inner):
                head = g * inner + i
                first = (index * inner + i) * rows
                heads_ref[
                    index * rows : (index + 1) * rows, head * HD : (head + 1) * HD
                ] = mixed[first : first + rows]


def project(heads_ref, w_ref, outs):
    rows, columns = outs[0].shape
    tile = min(COLUMN_TILE, columns)
    for first in range(0, columns, tile):
        here = slice(first, first + tile)
        product = jnp.dot(heads_ref[...], w_ref[:, here], preferred_element_type=jnp.float32)
        for index, out in enumerate(outs):
            out[:, here] = product[index * rows : (index + 1) * rows].astype(out.dtype)


def project_arriving(heads_ref, w_ref, outs, sum_ref, copies):
    rows, columns = outs[0].shape
    tile = min(COLUMN_TILE, columns)
    part_rows = w_ref.shape[0] // len(copies)
    for part, copy in enumerate(copies):
        copy.wait()
        depth = slice(part * part_rows, (part + 1) * part_rows)
        for first in range(0, columns, tile):
            here = slice(first, first + tile)
            product = jnp.dot(
                heads_ref[:, depth], w_ref[depth, here], preferred_element_type=jnp.float32
            )
            if part > 0:
                product = product + sum_ref[:, here]
            if part < len(copies) - 1:
                sum_ref[:, here] = product
            else:
                for index, out in enumerate(outs):
                    out[:, here] = product[index * rows : (index + 1) * rows].astype(out.dtype)


def held_copies(new_kv, cache_kv, out_weight, fresh_ref, cache_ref, w_ref, sem):
    kv_width = cache_ref.shape[2]
    heads_here = w_ref.shape[0] // HD
    kv_column = pl.multiple_of(lax.axis_index("head") * heads_here // GROUP * HD, HD)
    lanes = pl.ds(kv_column, kv_width)
    pairs = []
    for tick in range(fresh_ref.shape[0]):
        for part in range(2):
            pairs.append((new_kv.at[tick, part, :, lanes], fresh_ref.at[tick, part]))
    for part in range(2):
        pairs.append((cache_kv.at[part, :, lanes], cache_ref.at[part]))
    part_rows = w_ref.shape[0] // WEIGHT_PARTS
    for part in range(WEIGHT_PARTS):
        here = pl.ds(part * part_rows, part_rows)
        pairs.append((out_weight.at[0, here, :], w_ref.at[here, :]))
    copies = [
        pltpu.make_async_copy(source, target, sem.at[index])
        for index, (source, target) in enumerate(pairs)
    ]
    return copies[:-WEIGHT_PARTS], copies[-WEIGHT_PARTS:]


def first_kernel(
    ticks, rows, choose, active, lengths, queries, new_kv, cache_kv, out_weight, *rest
):
    outs = rest[: len(ticks)]
    fresh_ref, cache_ref, w_ref, length_ref, q_ref, heads_ref, sum_ref, sem = rest[len(ticks) :]
    z = lax.axis_index("head")

    @pl.when(active(z))
    def _():
        row_first = pl.multiple_of(choose(z) * rows, rows)
        copies, w_copies = held_copies(
            new_kv, cache_kv, out_weight, fresh_ref, cache_ref, w_ref, sem
        )
        used = len(copies) + len(w_copies)
        copies.append(pltpu.make_async_copy(lengths, length_ref, sem.at[used]))
        for index, tick in enumerate(ticks):
            copies.append(
                pltpu.make_async_copy(
                    queries.at[tick, pl.ds(row_first, rows), :],
                    q_ref.at[index],
                    sem.at[used + 1 + index],
                )
            )
        for copy in copies + w_copies:
            copy.start()
        for copy in copies:
            copy.wait()
        attend(
            ticks,
            rows,
            row_first,
            length_ref[lax.axis_index("section")],
            lambda index, lanes: q_ref[index, :, lanes],
            fresh_ref,
            cache_ref,
            heads_ref,
        )
        project_arriving(heads_ref, w_ref, outs, sum_ref, w_copies)


def later_rows(ticks, rows, choose, lengths, q_ref, fresh_ref, cache_ref, heads_ref):
    row_first = pl.multiple_of(choose(lax.axis_index("head")) * rows, rows)
    attend(
        ticks,
        rows,
        row_first,
        lengths[lax.axis_index("section")],
        lambda index, lanes: q_ref[ticks[index], pl.ds(row_first, rows), lanes],
        fresh_ref,
        cache_ref,
        heads_ref,
    )


def second_kernel(
    ticks,
    rows,
    choose,
    active,
    lengths,
    queries,
    new_kv,
    cache_kv,
    out_weight,
    residual,
    fresh_in,
    cache_in,
    w_in,
    dep,
    *rest,
):
    outs = rest[: len(ticks)]
    q_ref, by_tick_ref, fresh_ref, cache_ref, w_ref, *scratch = rest[len(ticks) :]
    heads_ref, residual_ref, sem, q_sem, residual_sem = scratch
    late = jnp.logical_not(active(lax.axis_index("head")))
    copies, w_copies = held_copies(new_kv, cache_kv, out_weight, fresh_ref, cache_ref, w_ref, sem)
    q_copy = pltpu.make_async_copy(queries, q_ref, q_sem)
    q_copy.start()
    residual_copy = pltpu.make_async_copy(residual, residual_ref, residual_sem)
    residual_copy.start()

    @pl.when(late)
    def _():
        for copy in copies + w_copies:
            copy.start()
        for copy in copies:
            copy.wait()

    q_copy.wait()
    later_rows(ticks, rows, choose, lengths, q_ref, fresh_ref, cache_ref, heads_ref)

    @pl.when(late)
    def _():
        for copy in w_copies:
            copy.wait()

    project(heads_ref, w_ref, outs)
    residual_copy.wait()
    for tick in range(by_tick_ref.shape[0]):
        by_tick_ref[tick] = residual_ref[:, tick, :]


def plus(left, right, out):
    out[...] = (left[...].astype(jnp.float32) + right[...].astype(jnp.float32)).astype(out.dtype)


def rows_kernel(ticks, rows, choose, active, names, *refs):
    ref = dict(zip(names, refs))
    if "out" in ref:
        outs = [ref["out"].at[index] for index in range(len(ticks))]
    else:
        outs = [ref["out%d" % index] for index in range(len(ticks))]

    @pl.when(active(lax.axis_index("head")))
    def _():
        later_rows(
            ticks, rows, choose, ref["lengths"], ref["q"], ref["fresh"], ref["cache"], ref["heads"]
        )
        project(ref["heads"], ref["w"], outs)
        if "residual" in ref:
            for index, out in enumerate(outs):
                plus(out, ref["residual"].at[index], out)


def in_vmem(array):
    return pltpu.with_memory_space_constraint(array, pltpu.VMEM)


def in_hbm(array):
    return pltpu.with_memory_space_constraint(array, pltpu.HBM)


WHOLE = pl.BlockSpec(memory_space=pltpu.VMEM)
ANYWHERE = pl.BlockSpec(memory_space=pl.ANY)
PARAMS = pltpu.CompilerParams(vmem_limit_bytes=28 * 2**20)
def cost_of(flops):
    return pl.CostEstimate(flops=flops, bytes_accessed=1000, transcendentals=0)


COST = cost_of(1000)
COST_OWN = cost_of(4 * 10**9)
COST_SUM = cost_of(4500 * 10**6)
COST_D = cost_of(4500 * 10**6)
COST_C = cost_of(4500 * 10**6)
LONG = cost_of(4 * 10**10)


def held_shapes(queries, new_kv, cache_kv, out_weight):
    tick_count, row_count, head_width = queries.shape
    kv_width = max(1, head_width // HD // GROUP) * HD
    kind = queries.dtype
    return [
        pltpu.VMEM((tick_count, 2, row_count, kv_width), kind),
        pltpu.VMEM((2, cache_kv.shape[1], kv_width), kind),
        pltpu.VMEM((head_width, out_weight.shape[2]), kind),
    ]


def first_rows(ticks, rows, choose, active, lengths, *arrays):
    queries, out_weight = arrays[0], arrays[3]
    tick_count, row_count, head_width = queries.shape
    columns = out_weight.shape[2]
    kind = queries.dtype
    out_shape = [pltpu.VMEM((rows, columns), kind)] * len(ticks) + held_shapes(*arrays)
    results = pl.pallas_call(
        functools.partial(first_kernel, ticks, rows, choose, active),
        out_shape=out_shape,
        in_specs=[ANYWHERE] * 5,
        out_specs=[WHOLE] * len(out_shape),
        scratch_shapes=[
            pltpu.SMEM(lengths.shape, lengths.dtype),
            pltpu.VMEM((len(ticks), rows, head_width), kind),
            pltpu.VMEM((len(ticks) * rows, head_width), kind),
            pltpu.VMEM((len(ticks) * rows, columns), jnp.float32),
            pltpu.SemaphoreType.DMA((3 + 2 * tick_count + WEIGHT_PARTS + len(ticks),)),
        ],
        compiler_params=PARAMS,
        cost_estimate=COST,
    )(*[in_hbm(array) for array in (lengths, *arrays)])
    return results[: len(ticks)], results[len(ticks) :]


def second_rows(ticks, rows, choose, active, lengths, arrays, residual, held, dep):
    queries, out_weight = arrays[0], arrays[3]
    tick_count, row_count, head_width = queries.shape
    kind = queries.dtype
    out_shape = [pltpu.VMEM((rows, out_weight.shape[2]), kind)] * len(ticks)
    out_shape += [
        pltpu.VMEM(queries.shape, kind),
        pltpu.VMEM((tick_count, residual.shape[0], residual.shape[2]), kind),
    ] + held_shapes(*arrays)
    results = pl.pallas_call(
        functools.partial(second_kernel, ticks, rows, choose, active),
        out_shape=out_shape,
        in_specs=[pl.BlockSpec(memory_space=pltpu.SMEM)] + [ANYWHERE] * 5 + [WHOLE] * 3 + [ANYWHERE],
        out_specs=[WHOLE] * len(out_shape),
        scratch_shapes=[
            pltpu.VMEM((len(ticks) * rows, head_width), kind),
            pltpu.VMEM(residual.shape, kind),
            pltpu.SemaphoreType.DMA((2 + 2 * tick_count + WEIGHT_PARTS,)),
            pltpu.SemaphoreType.DMA,
            pltpu.SemaphoreType.DMA,
        ],
        input_output_aliases={6 + index: len(ticks) + 2 + index for index in range(3)},
        compiler_params=PARAMS,
        cost_estimate=COST,
    )(
        lengths,
        *[in_hbm(array) for array in (*arrays, residual)],
        *[in_vmem(array) for array in held],
        dep,
    )
    here = len(ticks)
    return results[:here], results[here + 1], (lengths, results[here], *results[here + 2 :])


def project_rows(ticks, rows, choose, active, held, blocks, cost, deps, split=False):
    lengths, queries, fresh, cache, weight = held
    columns = weight.shape[1]
    kind = queries.dtype
    operands = {"q": queries, "fresh": fresh, "cache": cache, "w": weight}
    operands.update(blocks)
    if split:
        outs = {"out%d" % index: pltpu.VMEM((rows, columns), kind) for index in range(len(ticks))}
    else:
        outs = {"out": pltpu.VMEM((len(ticks), rows, columns), kind)}
    names = ["lengths"] + list(operands) + ["dep"] * len(deps) + list(outs) + ["heads"]
    return pl.pallas_call(
        functools.partial(rows_kernel, ticks, rows, choose, active, names),
        out_shape=list(outs.values()),
        in_specs=[pl.BlockSpec(memory_space=pltpu.SMEM)]
        + [WHOLE] * len(operands)
        + [ANYWHERE] * len(deps),
        out_specs=[WHOLE] * len(outs),
        scratch_shapes=[pltpu.VMEM((len(ticks) * rows, queries.shape[2]), kind)],
        compiler_params=PARAMS,
        cost_estimate=cost,
    )(lengths, *[in_vmem(array) for array in operands.values()], *deps)


def small_kernel(kernel, shape, kind, cost, *blocks, deps=()):
    return pl.pallas_call(
        kernel,
        out_shape=pltpu.VMEM(shape, kind),
        in_specs=[WHOLE] * len(blocks) + [ANYWHERE] * len(deps),
        out_specs=WHOLE,
        compiler_params=PARAMS,
        cost_estimate=cost,
    )(*blocks, *deps)


def add_kernel(left, right, *rest):
    plus(left, right, rest[-1])


def by_role_kernel(active, count, *refs):
    out = refs[-1]
    plain, left, right = refs[:count], refs[count : 2 * count], refs[2 * count : 3 * count]
    here = active(lax.axis_index("head"))

    @pl.when(here)
    def _():
        for index in range(count):
            plus(left[index], right[index], out.at[index])

    @pl.when(jnp.logical_not(here))
    def _():
        for index in range(count):
            out[index] = plain[index][...]


def whole_or_parts(refs, ticks):
    return [refs[0].at[index] for index in range(ticks)] if len(refs) == 1 else list(refs)


def outward_kernel(active, ticks, plain, left, *rest):
    refs = whole_or_parts([plain], ticks) + whole_or_parts([left], ticks) + list(rest[:ticks])
    by_role_kernel(active, ticks, *refs, rest[-1])


def inner_kernel(active, ticks, *refs):
    plain = list(refs[:ticks])
    left, right = refs[ticks], refs[ticks + 1]
    refs = plain + whole_or_parts([left], ticks) + whole_or_parts([right], ticks) + [refs[-1]]
    by_role_kernel(active, ticks, *refs)


def add_wide_kernel(ticks, block, *refs):
    out = refs[-1]
    for index in range(ticks):
        out[index] = block[index].astype(jnp.float32) + refs[index][...].astype(jnp.float32)


def finish_kernel(wide, block, out, buf, sem):
    step = 16
    copies = []
    for first in range(0, out.shape[0], step):
        here = pl.ds(first, step)
        for tick in range(out.shape[1]):
            total = wide[tick, here, :] + block[tick, here, :].astype(jnp.float32)
            buf[here, tick, :] = total.astype(out.dtype)
        copies.append(pltpu.make_async_copy(buf.at[here], out.at[here], sem.at[first // step]))
        copies[-1].start()
    for copy in copies:
        copy.wait()


def finish(wide, block):
    tick_count, rows, columns = block.shape
    shape = (rows, tick_count, columns)
    return pl.pallas_call(
        finish_kernel,
        out_shape=jax.ShapeDtypeStruct(shape, block.dtype),
        in_specs=[WHOLE] * 2,
        out_specs=ANYWHERE,
        scratch_shapes=[
            pltpu.VMEM(shape, block.dtype),
            pltpu.SemaphoreType.DMA((rows // 16,)),
        ],
        compiler_params=PARAMS,
        cost_estimate=COST,
    )(in_vmem(wide), in_vmem(block))


def add(left, right):
    return (left.astype(jnp.float32) + right.astype(jnp.float32)).astype(jnp.bfloat16)


def on_device(residual, queries, new_kv, cache_kv, lengths, out_weight):
    section_count = lax.axis_size("section")
    head_count = lax.axis_size("head")
    tick_count, row_count, head_width = queries.shape
    arrays = (queries, new_kv, cache_kv, out_weight)
    rows = row_count // head_count
    ticks = tuple(range(tick_count))

    def send(block, pairs, distance):
        route = [
            (s * head_count + a, (s + distance) % section_count * head_count + b)
            for s in range(section_count)
            for a, b in pairs
        ]
        return lax.ppermute(block, ("section", "head"), route)

    if head_count != 4 or tick_count != 2:
        partial, _ = first_rows(ticks, row_count, lambda z: 0, lambda z: z >= 0, lengths, *arrays)
        pieces = [
            lax.psum_scatter(block, "head", scatter_dimension=0, tiled=True) for block in partial
        ]
        updated = add(residual, jnp.stack(pieces, axis=1))
        return send(updated, [(i, i) for i in range(head_count)], 1)

    ends = [(0, 1), (3, 2)]
    middle = [(1, 2), (2, 1)]
    outward = [(0, 1), (3, 2), (1, 0), (2, 3)]

    def first(z):
        return jnp.where(z < 2, 3, 0)

    def second(z):
        return jnp.where(z < 2, 2, 1)

    def third(z):
        return jnp.where(z == 0, 1, jnp.where(z == 1, 0, jnp.where(z == 2, 3, 2)))

    def at_end(z):
        return (z == 0) | (z == head_count - 1)

    def in_middle(z):
        return jnp.logical_not(at_end(z))

    def third_or_second(z):
        return jnp.where(at_end(z), third(z), second(z))

    def everywhere(z):
        return z >= 0

    (a0_early,), loaded = first_rows((0,), rows, first, at_end, lengths, *arrays)
    a0_far = send(a0_early, ends, 0)
    (a0, a1), own_residual, held = second_rows(
        ticks, rows, first, at_end, lengths, arrays, residual, loaded, a0_early
    )
    a1_far = send(a1, ends, 0)
    (b,) = project_rows(ticks, rows, second, at_end, held, {}, COST, [a1])
    b_far = send(b, ends, 0)
    a0_sum = small_kernel(add_kernel, a0.shape, a0.dtype, COST, a0, a0_far, deps=[b])
    a0_mid = send(a0_sum, middle, 0)
    own = project_rows(
        ticks,
        rows,
        lambda z: z,
        everywhere,
        held,
        {"residual": own_residual},
        COST_OWN,
        [a0_sum],
        split=True,
    )
    own_here = [send(block, [(1, 1), (2, 2)], 1) for block in own]
    a1_sum = small_kernel(add_kernel, a1.shape, a1.dtype, COST_SUM, a1, a1_far, deps=[own[0]])
    a1_mid = send(a1_sum, middle, 0)
    (d,) = project_rows(
        ticks, rows, third_or_second, everywhere, held, {}, COST_D, [a1_sum, a0_mid]
    )
    (c,) = project_rows(ticks, rows, third, in_middle, held, {}, COST_C, [d])
    c_sum = small_kernel(
        functools.partial(outward_kernel, in_middle, tick_count),
        c.shape,
        c.dtype,
        COST,
        d,
        c,
        a0_mid,
        a1_mid,
        deps=own_here,
    )
    c_here = send(c_sum, outward, 1)
    d_sum = small_kernel(
        functools.partial(inner_kernel, in_middle, tick_count),
        d.shape,
        d.dtype,
        COST,
        *own,
        d,
        b_far,
        deps=[c_sum],
    )
    d_here = send(d_sum, middle + [(0, 0), (3, 3)], 1)
    wide = small_kernel(
        functools.partial(add_wide_kernel, tick_count),
        c.shape,
        jnp.float32,
        LONG,
        c_here,
        *own_here,
    )
    return finish(wide, d_here)


def solution(mesh):
    placed = (
        P(("section", "head"), None, None),
        P(None, "section", "head"),
        P(None, None, "section", None),
        P(None, "section", None),
        P(),
        P("section", "head", None),
    )
    return jax.shard_map(
        on_device,
        mesh=mesh,
        in_specs=placed,
        out_specs=P(("section", "head"), None, None),
        check_vma=False,
    )
```

time: 88.4 us -> 84.2 us (0.952)
  Pallas kernels: 28.6 us -> 32.5 us
  starting transfers between devices: 16.8 us -> 13.5 us
  local copies, waits for them, and re-layouts: 2.73 us -> 0.01 us
  other arithmetic: 1.44 us -> 0 us
    pallas_call x10 -> x12, Pallas kernels: 28.6 us -> 32.5 us  [the longest x4 18 us: project_rows(): pl.pallas_call(functools.partial(rows_kernel, ticks, rows, choose, active...]
    ppermute x10 -> x9, starting transfers between devices: 16.8 us -> 13.5 us  [send(): return lax.ppermute(block, ('section', 'head'), route)]
    transpose x1 -> x0, local copies, waits for them, and re-layouts: 2.06 us -> none  [on_device(): return total.astype(jnp.bfloat16).transpose(1, 0, 2)]
    ppermute x10 -> x9, waiting for transfers between devices: 37.7 us -> 37.7 us  [send(): return lax.ppermute(block, ('section', 'head'), route)]
  transfers between devices with their start and end apart: 10 -> 9, of which waited for: 8 -> 5; matrix products, arithmetic and copies ran while one was open for 1% -> 0% of each run, Pallas kernels for 25% -> 37%
where the time goes in v1:
time: 84.2 us; the launch traced here: 84 us
  waiting for transfers between devices  37.7 us (45%)
  Pallas kernels  32.5 us (39%)
  starting transfers between devices  13.5 us (16%)
    ppermute x9, waiting for transfers between devices, send(): return lax.ppermute(block, ('section', 'head'), route)  37.7 us
    pallas_call x4, Pallas kernels, project_rows(): pl.pallas_call(functools.partial(rows_kernel, ticks, rows, choose, active...  18 us
    ppermute x9, starting transfers between devices, send(): return lax.ppermute(block, ('section', 'head'), route)  13.5 us
    pallas_call x1, Pallas kernels, second_rows(): pl.pallas_call(functools.partial(second_kernel, ticks, rows, choose, acti...  12 us
  transfers between devices with their start and end apart: 9, of which 5 were waited for; matrix products, arithmetic and copies ran while one was open for 0% of the time, Pallas kernels for 37%

profile of v1, /device:TPU:16, one launch (start us, length us, event | category | flops | bytes accessed | tf_op | source)
XLA Modules:
  0.0 84.0 jit_solution(4043095433104107837)
XLA Ops:
  0.0 0.0 copy-start
  0.0 0.1 shard_map.64
  0.1 1.3 %collective-permute-start.1 = (bf16[64,4096]{1,0:T(8,128)(2,1)S(1)}, bf16[64,4096]{1,0:T(8,128)(2,1)S(1)}, u32[]{:S(2)}, u32[]{:S(2)}) collective-permute-start(bf16[64,4096]{1,0:T(8,128)(2,1)S(1)} %get-tuple-element.21.dep), channel_id=1, source_target_pairs={{0,1},{3,2},{4,5},{7,6},{8,9},{11,10},{12,13},{15,14},{16,17},{19,... | collective-permute-start | bytes 1572872 | tf_op jit(solution)/shard_map/ppermute | solution.py:484
  1.4 0.0 copy-done
  1.4 12.0 %shard_map.65 = (bf16[64,4096]{1,0:T(8,128)(2,1)S(1)}, bf16[64,4096]{1,0:T(8,128)(2,1)S(1)}, bf16[2,256,1024]{2,1,0:T(8,128)(2,1)S(1)}, bf16[2,64,4096]{2,1,0:T(...) custom-call(s32[8]{0:T(128)S(1)} %copy-done, ...), custom_call_target="tpu_custom_call", output_to_operand_aliasing={{4}: (6, {}), {5}: (7, {}), {6}: (8, {})} | custom-call | flops 1000 | bytes 1000 | tf_op jit(solution)/shard_map/pallas_call | solution.py:333
  13.5 1.3 %collective-permute-start = (bf16[64,4096]{1,0:T(8,128)(2,1)S(1)}, bf16[64,4096]{1,0:T(8,128)(2,1)S(1)}, u32[]{:S(2)}, u32[]{:S(2)}) collective-permute-start(bf16[64,4096]{1,0:T(8,128)(2,1)S(1)} %get-tuple-element.26.refs_5_.left), channel_id=1, source_target_pairs={{0,1},{3,2},{4,5},{7,6},{8,9},{11,10},{12,13},{15,14},{16,17},{19,... | collective-permute-start | bytes 1572872 | tf_op jit(solution)/shard_map/ppermute | solution.py:484
  14.8 0.7 shard_map.66.rest_0_
  15.5 1.3 %collective-permute-start.7 = (bf16[2,64,4096]{2,1,0:T(8,128)(2,1)S(1)}, bf16[2,64,4096]{2,1,0:T(8,128)(2,1)S(1)}, u32[]{:S(2)}, u32[]{:S(2)}) collective-permute-start(bf16[2,64,4096]{2,1,0:T(8,128)(2,1)S(1)} %shard_map.66.rest_0_), channel_id=1, source_target_pairs={{0,1},{3,2},{4,5},{7,6},{8,9},{11,10},{12,13},{15,14},{16,17},{19,... | collective-permute-start | bytes 3145736 | tf_op jit(solution)/shard_map/ppermute | solution.py:484
  16.8 4.8 %collective-permute-done.1.right = bf16[64,4096]{1,0:T(8,128)(2,1)S(1)} collective-permute-done((bf16[64,4096]{1,0:T(8,128)(2,1)S(1)}, bf16[64,4096]{1,0:T(8,128)(2,1)S(1)}, u32[]{:S(2)}, u32[]{:S(2)}) %collective-permute-start.1) | collective-permute-done | bytes 524320 | tf_op jit(solution)/shard_map/ppermute | solution.py:484
  21.6 0.1 shard_map.67.refs_6_
  21.7 1.9 %collective-permute-start.2 = (bf16[64,4096]{1,0:T(8,128)(2,1)S(1)}, bf16[64,4096]{1,0:T(8,128)(2,1)S(1)}, u32[]{:S(2)}, u32[]{:S(2)}) collective-permute-start(bf16[64,4096]{1,0:T(8,128)(2,1)S(1)} %shard_map.67.refs_6_), channel_id=1, source_target_pairs={{1,2},{2,1},{5,6},{6,5},{9,10},{10,9},{13,14},{14,13},{17,18},{18,... | collective-permute-start | bytes 1572872 | tf_op jit(solution)/shard_map/ppermute | solution.py:484
  23.6 5.7 %shard_map.68 = (bf16[64,4096]{1,0:T(8,128)(2,1)S(1)}, bf16[64,4096]{1,0:T(8,128)(2,1)S(1)}) custom-call(s32[8]{0:T(128)S(1)} %copy-done, bf16[2,256,1024]{2,1,0:T(8,128)(2,1)S(1)} %get-tuple-element.22.refs_1_, bf16[2,2,256,256]{3,2,1,0:T(8,128)(2,1)S(1)} %get-tuple-element.23.refs_2_, bf16[2,1536,256]{2,1,0:T(8,128)(2,1)S(1)} %get-tuple-element.24.refs_3_, ...), custom_call_target="tpu_custom_call" | custom-call | flops 4000000000 | bytes 1000 | tf_op jit(solution)/shard_map/pallas_call | solution.py:369
  29.4 1.9 %collective-permute-start.4 = (bf16[64,4096]{1,0:T(8,128)(2,1)S(1)}, bf16[64,4096]{1,0:T(8,128)(2,1)S(1)}, u32[]{:S(2)}, u32[]{:S(2)}) collective-permute-start(bf16[64,4096]{1,0:T(8,128)(2,1)S(1)} %get-tuple-element.29.rest_0_.refs_0_), channel_id=1, source_target_pairs={{1,5},{2,6},{5,9},{6,10},{9,13},{10,14},{13,17},{14,18},{17,21},{1... | collective-permute-start | bytes 1572872 | tf_op jit(solution)/shard_map/ppermute | solution.py:484
  31.3 1.5 %collective-permute-done.right = bf16[64,4096]{1,0:T(8,128)(2,1)S(1)} collective-permute-done((bf16[64,4096]{1,0:T(8,128)(2,1)S(1)}, bf16[64,4096]{1,0:T(8,128)(2,1)S(1)}, u32[]{:S(2)}, u32[]{:S(2)}) %collective-permute-start) | collective-permute-done | bytes 524320 | tf_op jit(solution)/shard_map/ppermute | solution.py:484
  32.8 0.1 shard_map.69.refs_5_
  32.9 2.4 %collective-permute-start.3 = (bf16[64,4096]{1,0:T(8,128)(2,1)S(1)}, bf16[64,4096]{1,0:T(8,128)(2,1)S(1)}, u32[]{:S(2)}, u32[]{:S(2)}) collective-permute-start(bf16[64,4096]{1,0:T(8,128)(2,1)S(1)} %shard_map.69.refs_5_), channel_id=1, source_target_pairs={{1,2},{2,1},{5,6},{6,5},{9,10},{10,9},{13,14},{14,13},{17,18},{18,... | collective-permute-start | bytes 1572872 | tf_op jit(solution)/shard_map/ppermute | solution.py:484
  35.4 3.2 %collective-permute-start.5 = (bf16[64,4096]{1,0:T(8,128)(2,1)S(1)}, bf16[64,4096]{1,0:T(8,128)(2,1)S(1)}, u32[]{:S(2)}, u32[]{:S(2)}) collective-permute-start(bf16[64,4096]{1,0:T(8,128)(2,1)S(1)} %get-tuple-element.30.refs_1_), channel_id=1, source_target_pairs={{1,5},{2,6},{5,9},{6,10},{9,13},{10,14},{13,17},{14,18},{17,21},{1... | collective-permute-start | bytes 1572872 | tf_op jit(solution)/shard_map/ppermute | solution.py:484
  38.6 0.0 collective-permute-done.2.refs_6_.rest_0_
  38.6 5.9 %shard_map.70.refs_5_.plain.refs_2_ = bf16[2,64,4096]{2,1,0:T(8,128)(2,1)S(1)} custom-call(s32[8]{0:T(128)S(1)} %copy-done, bf16[2,256,1024]{2,1,0:T(8,128)(2,1)S(1)} %get-tuple-element.22.refs_1_, bf16[2,2,256,256]{3,2,1,0:T(8,128)(2,1)S(1)} %get-tuple-element.23.refs_2_, bf16[2,1536,256]{2,1,0:T(8,128)(2,1)S(1)} %get-tuple-element.24.refs_3_, ...), custom_call_target="tpu_custom_call" | custom-call | flops 4499999744 | bytes 1000 | tf_op jit(solution)/shard_map/pallas_call | solution.py:369
  44.5 5.7 %shard_map.71.left = bf16[2,64,4096]{2,1,0:T(8,128)(2,1)S(1)} custom-call(s32[8]{0:T(128)S(1)} %copy-done, bf16[2,256,1024]{2,1,0:T(8,128)(2,1)S(1)} %get-tuple-element.22.refs_1_, bf16[2,2,256,256]{3,2,1,0:T(8,128)(2,1)S(1)} %get-tuple-element.23.refs_2_, bf16[2,1536,256]{2,1,0:T(8,128)(2,1)S(1)} %get-tuple-element.24.refs_3_, ...), custom_call_target="tpu_custom_call" | custom-call | flops 4499999744 | bytes 1000 | tf_op jit(solution)/shard_map/pallas_call | solution.py:369
  50.2 0.0 collective-permute-done.3.rest_1_
  50.2 0.0 collective-permute-done.4.rest_2_.refs_0_
  50.2 0.0 collective-permute-done.5.rest_3_.refs_1_
  50.2 0.3 shard_map.72.refs_4_
  50.5 0.1 collective-permute-start.6
  50.5 4.7 %collective-permute-done.7.refs_3_ = bf16[2,64,4096]{2,1,0:T(8,128)(2,1)S(1)} collective-permute-done((bf16[2,64,4096]{2,1,0:T(8,128)(2,1)S(1)}, bf16[2,64,4096]{2,1,0:T(8,128)(2,1)S(1)}, u32[]{:S(2)}, u32[]{:S(2)}) %collective-permute-start.7) | collective-permute-done | bytes 1048608 | tf_op jit(solution)/shard_map/ppermute | solution.py:484
  55.3 0.2 shard_map.74
  55.5 0.1 collective-permute-start.8
  55.6 23.4 %collective-permute-done.6.block = bf16[2,64,4096]{2,1,0:T(8,128)(2,1)S(1)} collective-permute-done((bf16[2,64,4096]{2,1,0:T(8,128)(2,1)S(1)}, bf16[2,64,4096]{2,1,0:T(8,128)(2,1)S(1)}, u32[]{:S(2)}, u32[]{:S(2)}) %collective-permute-start.6) | collective-permute-done | bytes 1048608 | tf_op jit(solution)/shard_map/ppermute | solution.py:484
  78.9 0.2 shard_map.73.wide
  79.2 3.3 %collective-permute-done.8.block = bf16[2,64,4096]{2,1,0:T(8,128)(2,1)S(1)} collective-permute-done((bf16[2,64,4096]{2,1,0:T(8,128)(2,1)S(1)}, bf16[2,64,4096]{2,1,0:T(8,128)(2,1)S(1)}, u32[]{:S(2)}, u32[]{:S(2)}) %collective-permute-start.8) | collective-permute-done | bytes 1048608 | tf_op jit(solution)/shard_map/ppermute | solution.py:484
  82.5 1.3 %shard_map.75 = bf16[64,2,4096]{2,1,0:T(2,128)(2,1)} custom-call(f32[2,64,4096]{2,1,0:T(8,128)S(1)} %shard_map.73.wide, bf16[2,64,4096]{2,1,0:T(8,128)(2,1)S(1)} %collective-permute-done.8.block), custom_call_target="tpu_custom_call" | custom-call | flops 1000 | bytes 1000 | tf_op jit(solution)/shard_map/pallas_call | solution.py:452
Async XLA Ops:
  0.0 1.4 %copy-start = (s32[8]{0:T(128)S(1)}, s32[8]{0:T(128)}, u32[]{:S(2)}) copy-start(s32[8]{0:T(128)} %refs_0_.7) | copy-start | bytes 100
  0.1 21.5 %collective-permute-start.1 = (bf16[64,4096]{1,0:T(8,128)(2,1)S(1)}, bf16[64,4096]{1,0:T(8,128)(2,1)S(1)}, u32[]{:S(2)}, u32[]{:S(2)}) collective-permute-start(bf16[64,4096]{1,0:T(8,128)(2,1)S(1)} %get-tuple-element.21.dep), channel_id=1, source_target_pairs={{0,1},{3,2},{4,5},{7,6},{8,9},{11,10},{12,13},{15,14},{16,17},{19,... | collective-permute-start | bytes 1572872 | tf_op jit(solution)/shard_map/ppermute | solution.py:484
  13.5 19.3 %collective-permute-start = (bf16[64,4096]{1,0:T(8,128)(2,1)S(1)}, bf16[64,4096]{1,0:T(8,128)(2,1)S(1)}, u32[]{:S(2)}, u32[]{:S(2)}) collective-permute-start(bf16[64,4096]{1,0:T(8,128)(2,1)S(1)} %get-tuple-element.26.refs_5_.left), channel_id=1, source_target_pairs={{0,1},{3,2},{4,5},{7,6},{8,9},{11,10},{12,13},{15,14},{16,17},{19,... | collective-permute-start | bytes 1572872 | tf_op jit(solution)/shard_map/ppermute | solution.py:484
  15.5 39.8 %collective-permute-start.7 = (bf16[2,64,4096]{2,1,0:T(8,128)(2,1)S(1)}, bf16[2,64,4096]{2,1,0:T(8,128)(2,1)S(1)}, u32[]{:S(2)}, u32[]{:S(2)}) collective-permute-start(bf16[2,64,4096]{2,1,0:T(8,128)(2,1)S(1)} %shard_map.66.rest_0_), channel_id=1, source_target_pairs={{0,1},{3,2},{4,5},{7,6},{8,9},{11,10},{12,13},{15,14},{16,17},{19,... | collective-permute-start | bytes 3145736 | tf_op jit(solution)/shard_map/ppermute | solution.py:484
  21.7 16.9 %collective-permute-start.2 = (bf16[64,4096]{1,0:T(8,128)(2,1)S(1)}, bf16[64,4096]{1,0:T(8,128)(2,1)S(1)}, u32[]{:S(2)}, u32[]{:S(2)}) collective-permute-start(bf16[64,4096]{1,0:T(8,128)(2,1)S(1)} %shard_map.67.refs_6_), channel_id=1, source_target_pairs={{1,2},{2,1},{5,6},{6,5},{9,10},{10,9},{13,14},{14,13},{17,18},{18,... | collective-permute-start | bytes 1572872 | tf_op jit(solution)/shard_map/ppermute | solution.py:484
  29.4 20.8 %collective-permute-start.4 = (bf16[64,4096]{1,0:T(8,128)(2,1)S(1)}, bf16[64,4096]{1,0:T(8,128)(2,1)S(1)}, u32[]{:S(2)}, u32[]{:S(2)}) collective-permute-start(bf16[64,4096]{1,0:T(8,128)(2,1)S(1)} %get-tuple-element.29.rest_0_.refs_0_), channel_id=1, source_target_pairs={{1,5},{2,6},{5,9},{6,10},{9,13},{10,14},{13,17},{14,18},{17,21},{1... | collective-permute-start | bytes 1572872 | tf_op jit(solution)/shard_map/ppermute | solution.py:484
  32.9 17.3 %collective-permute-start.3 = (bf16[64,4096]{1,0:T(8,128)(2,1)S(1)}, bf16[64,4096]{1,0:T(8,128)(2,1)S(1)}, u32[]{:S(2)}, u32[]{:S(2)}) collective-permute-start(bf16[64,4096]{1,0:T(8,128)(2,1)S(1)} %shard_map.69.refs_5_), channel_id=1, source_target_pairs={{1,2},{2,1},{5,6},{6,5},{9,10},{10,9},{13,14},{14,13},{17,18},{18,... | collective-permute-start | bytes 1572872 | tf_op jit(solution)/shard_map/ppermute | solution.py:484
  35.4 14.8 %collective-permute-start.5 = (bf16[64,4096]{1,0:T(8,128)(2,1)S(1)}, bf16[64,4096]{1,0:T(8,128)(2,1)S(1)}, u32[]{:S(2)}, u32[]{:S(2)}) collective-permute-start(bf16[64,4096]{1,0:T(8,128)(2,1)S(1)} %get-tuple-element.30.refs_1_), channel_id=1, source_target_pairs={{1,5},{2,6},{5,9},{6,10},{9,13},{10,14},{13,17},{14,18},{17,21},{1... | collective-permute-start | bytes 1572872 | tf_op jit(solution)/shard_map/ppermute | solution.py:484
  50.5 28.5 %collective-permute-start.6 = (bf16[2,64,4096]{2,1,0:T(8,128)(2,1)S(1)}, bf16[2,64,4096]{2,1,0:T(8,128)(2,1)S(1)}, u32[]{:S(2)}, u32[]{:S(2)}) collective-permute-start(bf16[2,64,4096]{2,1,0:T(8,128)(2,1)S(1)} %shard_map.72.refs_4_), channel_id=1, source_target_pairs={{0,5},{3,6},{1,4},{2,7},{4,9},{7,10},{5,8},{6,11},{8,13},{11,14},{... | collective-permute-start | bytes 3145736 | tf_op jit(solution)/shard_map/ppermute | solution.py:484
  55.5 26.9 %collective-permute-start.8 = (bf16[2,64,4096]{2,1,0:T(8,128)(2,1)S(1)}, bf16[2,64,4096]{2,1,0:T(8,128)(2,1)S(1)}, u32[]{:S(2)}, u32[]{:S(2)}) collective-permute-start(bf16[2,64,4096]{2,1,0:T(8,128)(2,1)S(1)} %shard_map.74), channel_id=1, source_target_pairs={{1,6},{2,5},{0,4},{3,7},{5,10},{6,9},{4,8},{7,11},{9,14},{10,13},{... | collective-permute-start | bytes 3145736 | tf_op jit(solution)/shard_map/ppermute | solution.py:484

commit v2 on v1

--- a/solution.py
+++ b/solution.py
@@ -61,8 +61,8 @@
         for block in range(capacity // key_block):
             here = slice(block * key_block, (block + 1) * key_block)
             scores = scores_of(query_rows, cache_ref[0, here, lanes])
-            column = lax.broadcasted_iota(jnp.int32, scores.shape, 1)
-            scores = jnp.where(column < my_length - block * key_block, scores, neg_large)
+            column = lax.broadcasted_iota(jnp.int32, (1, key_block), 1)
+            scores = scores + jnp.where(column < my_length - block * key_block, 0.0, neg_large)
             blocks.append((scores, cache_ref[1, here, lanes]))
         highest = None
         for scores, _ in blocks:
@@ -162,10 +162,13 @@
                     sem.at[used + 1 + index],
                 )
             )
-        for copy in copies + w_copies:
+        early = len(w_copies) // 2
+        for copy in copies + w_copies[:early]:
             copy.start()
         for copy in copies:
             copy.wait()
+        for copy in w_copies[early:]:
+            copy.start()
         attend(
             ticks,
             rows,
@@ -245,22 +248,19 @@
     out[...] = (left[...].astype(jnp.float32) + right[...].astype(jnp.float32)).astype(out.dtype)
 
 
-def rows_kernel(ticks, rows, choose, active, names, *refs):
+def rows_kernel(ticks, rows, choose, names, *refs):
     ref = dict(zip(names, refs))
     if "out" in ref:
         outs = [ref["out"].at[index] for index in range(len(ticks))]
     else:
-        outs = [ref["out%d" % index] for index in range(len(ticks))]
-
-    @pl.when(active(lax.axis_index("head")))
-    def _():
-        later_rows(
-            ticks, rows, choose, ref["lengths"], ref["q"], ref["fresh"], ref["cache"], ref["heads"]
-        )
-        project(ref["heads"], ref["w"], outs)
-        if "residual" in ref:
-            for index, out in enumerate(outs):
-                plus(out, ref["residual"].at[index], out)
+        outs = [ref["out%d" % tick] for tick in ticks]
+    later_rows(
+        ticks, rows, choose, ref["lengths"], ref["q"], ref["fresh"], ref["cache"], ref["heads"]
+    )
+    project(ref["heads"], ref["w"], outs)
+    if "residual" in ref:
+        for index, out in enumerate(outs):
+            plus(out, ref["residual"].at[index], out)
 
 
 def in_vmem(array):
@@ -279,11 +279,13 @@
 
 
 COST = cost_of(1000)
-COST_OWN = cost_of(4 * 10**9)
-COST_SUM = cost_of(4500 * 10**6)
-COST_D = cost_of(4500 * 10**6)
-COST_C = cost_of(4500 * 10**6)
-LONG = cost_of(4 * 10**10)
+COST_X = cost_of(1000)
+COST_Y = cost_of(4500000000)
+COST_SUM = cost_of(1000)
+COST_V = cost_of(1000)
+COST_CS = cost_of(1000)
+COST_W = cost_of(1000)
+COST_D = [cost_of(4500000000), cost_of(1000)]
 
 
 def held_shapes(queries, new_kv, cache_kv, out_weight):
@@ -355,19 +357,21 @@
     return results[:here], results[here + 1], (lengths, results[here], *results[here + 2 :])
 
 
-def project_rows(ticks, rows, choose, active, held, blocks, cost, deps, split=False):
+def project_rows(ticks, rows, choose, held, cost, deps, residual=None, split=True):
     lengths, queries, fresh, cache, weight = held
     columns = weight.shape[1]
     kind = queries.dtype
     operands = {"q": queries, "fresh": fresh, "cache": cache, "w": weight}
-    operands.update(blocks)
+    if residual is not None:
+        operands["residual"] = residual
+    names = ["lengths"] + list(operands) + ["dep"] * len(deps)
     if split:
-        outs = {"out%d" % index: pltpu.VMEM((rows, columns), kind) for index in range(len(ticks))}
+        outs = {"out%d" % tick: pltpu.VMEM((rows, columns), kind) for tick in ticks}
     else:
         outs = {"out": pltpu.VMEM((len(ticks), rows, columns), kind)}
-    names = ["lengths"] + list(operands) + ["dep"] * len(deps) + list(outs) + ["heads"]
+    names += list(outs) + ["heads"]
     return pl.pallas_call(
-        functools.partial(rows_kernel, ticks, rows, choose, active, names),
+        functools.partial(rows_kernel, ticks, rows, choose, names),
         out_shape=list(outs.values()),
         in_specs=[pl.BlockSpec(memory_space=pltpu.SMEM)]
         + [WHOLE] * len(operands)
@@ -410,26 +414,23 @@
             out[index] = plain[index][...]
 
 
-def whole_or_parts(refs, ticks):
-    return [refs[0].at[index] for index in range(ticks)] if len(refs) == 1 else list(refs)
-
-
-def outward_kernel(active, ticks, plain, left, *rest):
-    refs = whole_or_parts([plain], ticks) + whole_or_parts([left], ticks) + list(rest[:ticks])
-    by_role_kernel(active, ticks, *refs, rest[-1])
-
-
-def inner_kernel(active, ticks, *refs):
-    plain = list(refs[:ticks])
-    left, right = refs[ticks], refs[ticks + 1]
-    refs = plain + whole_or_parts([left], ticks) + whole_or_parts([right], ticks) + [refs[-1]]
-    by_role_kernel(active, ticks, *refs)
-
-
-def add_wide_kernel(ticks, block, *refs):
+def inner_kernel(active, tick, plain, left, right, *rest):
+    out = rest[-1]
+    here = active(lax.axis_index("head"))
+
+    @pl.when(here)
+    def _():
+        plus(left, right, out)
+
+    @pl.when(jnp.logical_not(here))
+    def _():
+        out[...] = plain[tick]
+
+
+def wide_kernel(block, *refs):
     out = refs[-1]
-    for index in range(ticks):
-        out[index] = block[index].astype(jnp.float32) + refs[index][...].astype(jnp.float32)
+    for tick in range(out.shape[0]):
+        out[tick] = block[tick].astype(jnp.float32) + refs[tick][...].astype(jnp.float32)
 
 
 def finish_kernel(wide, block, out, buf, sem):
@@ -447,7 +448,7 @@
 
 
 def finish(wide, block):
-    tick_count, rows, columns = block.shape
+    tick_count, rows, columns = wide.shape
     shape = (rows, tick_count, columns)
     return pl.pallas_call(
         finish_kernel,
@@ -510,11 +511,8 @@
     def in_middle(z):
         return jnp.logical_not(at_end(z))
 
-    def third_or_second(z):
-        return jnp.where(at_end(z), third(z), second(z))
-
-    def everywhere(z):
-        return z >= 0
+    def by_role(at_ends, in_the_middle):
+        return lambda z: jnp.where(at_end(z), at_ends(z), in_the_middle(z))
 
     (a0_early,), loaded = first_rows((0,), rows, first, at_end, lengths, *arrays)
     a0_far = send(a0_early, ends, 0)
@@ -522,60 +520,48 @@
         ticks, rows, first, at_end, lengths, arrays, residual, loaded, a0_early
     )
     a1_far = send(a1, ends, 0)
-    (b,) = project_rows(ticks, rows, second, at_end, held, {}, COST, [a1])
-    b_far = send(b, ends, 0)
-    a0_sum = small_kernel(add_kernel, a0.shape, a0.dtype, COST, a0, a0_far, deps=[b])
+    x = project_rows(ticks, rows, by_role(second, third), held, COST_X, [a1])
+    x_far = [send(block, ends, 0) for block in x]
+    a0_sum = small_kernel(add_kernel, a0.shape, a0.dtype, COST, a0, a0_far, deps=[x[0]])
     a0_mid = send(a0_sum, middle, 0)
-    own = project_rows(
-        ticks,
-        rows,
-        lambda z: z,
-        everywhere,
-        held,
-        {"residual": own_residual},
-        COST_OWN,
-        [a0_sum],
-        split=True,
-    )
-    own_here = [send(block, [(1, 1), (2, 2)], 1) for block in own]
-    a1_sum = small_kernel(add_kernel, a1.shape, a1.dtype, COST_SUM, a1, a1_far, deps=[own[0]])
+    (y,) = project_rows(
+        ticks, rows, lambda z: z, held, COST_Y, [a0_sum], own_residual, split=False
+    )
+    y_here = send(y, [(1, 1), (2, 2)], 1)
+    a1_sum = small_kernel(add_kernel, a1.shape, a1.dtype, COST_SUM, a1, a1_far, deps=[y])
     a1_mid = send(a1_sum, middle, 0)
-    (d,) = project_rows(
-        ticks, rows, third_or_second, everywhere, held, {}, COST_D, [a1_sum, a0_mid]
-    )
-    (c,) = project_rows(ticks, rows, third, in_middle, held, {}, COST_C, [d])
+    v = project_rows(
+        ticks, rows, by_role(third, second), held, COST_V, [a1_sum, a0_mid, x_far[0]]
+    )
+    both = (tick_count,) + a0.shape
     c_sum = small_kernel(
-        functools.partial(outward_kernel, in_middle, tick_count),
-        c.shape,
-        c.dtype,
-        COST,
-        d,
-        c,
+        functools.partial(by_role_kernel, in_middle, tick_count),
+        both,
+        a0.dtype,
+        COST_CS,
+        *v,
+        *x,
         a0_mid,
         a1_mid,
-        deps=own_here,
     )
     c_here = send(c_sum, outward, 1)
-    d_sum = small_kernel(
-        functools.partial(inner_kernel, in_middle, tick_count),
-        d.shape,
-        d.dtype,
-        COST,
-        *own,
-        d,
-        b_far,
-        deps=[c_sum],
-    )
-    d_here = send(d_sum, middle + [(0, 0), (3, 3)], 1)
-    wide = small_kernel(
-        functools.partial(add_wide_kernel, tick_count),
-        c.shape,
-        jnp.float32,
-        LONG,
-        c_here,
-        *own_here,
-    )
-    return finish(wide, d_here)
+    d_here = []
+    deps = [c_sum]
+    for tick in ticks:
+        d_sum = small_kernel(
+            functools.partial(inner_kernel, in_middle, tick),
+            a0.shape,
+            a0.dtype,
+            COST_D[tick],
+            y,
+            v[tick],
+            x_far[tick],
+            deps=deps,
+        )
+        d_here.append(send(d_sum, middle + [(0, 0), (3, 3)], 1))
+        deps = [c_sum, y_here]
+    wide = small_kernel(wide_kernel, both, jnp.float32, COST_W, y_here, *d_here)
+    return finish(wide, c_here)
 
 
 def solution(mesh):

time: 84.2 us -> 80.4 us (0.955)
  Pallas kernels: 32.5 us -> 31 us
  waiting for transfers between devices: 37.7 us -> 36.4 us
  starting transfers between devices: 13.5 us -> 12.5 us
    pallas_call x4 -> x3, Pallas kernels: 18 us -> 16.7 us  [project_rows(): pl.pallas_call(functools.partial(rows_kernel, ticks, rows, choose, names)...]
    ppermute x9 -> x10, waiting for transfers between devices: 37.7 us -> 36.4 us  [send(): return lax.ppermute(block, ('section', 'head'), route)]
    ppermute x9 -> x10, starting transfers between devices: 13.5 us -> 12.5 us  [send(): return lax.ppermute(block, ('section', 'head'), route)]
  transfers between devices with their start and end apart: 9 -> 10, of which waited for: 5 -> 6; matrix products, arithmetic and copies ran while one was open for 0% -> 0% of each run, Pallas kernels for 37% -> 37%
where the time goes in v2:
time: 80.4 us; the launch traced here: 80.2 us
  waiting for transfers between devices  36.4 us (45%)
  Pallas kernels  31 us (39%)
  starting transfers between devices  12.5 us (16%)
    ppermute x10, waiting for transfers between devices, send(): return lax.ppermute(block, ('section', 'head'), route)  36.4 us
    pallas_call x3, Pallas kernels, project_rows(): pl.pallas_call(functools.partial(rows_kernel, ticks, rows, choose, names)...  16.7 us
    ppermute x10, starting transfers between devices, send(): return lax.ppermute(block, ('section', 'head'), route)  12.5 us
    pallas_call x1, Pallas kernels, second_rows(): pl.pallas_call(functools.partial(second_kernel, ticks, rows, choose, acti...  11.9 us
  transfers between devices with their start and end apart: 10, of which 6 were waited for; matrix products, arithmetic and copies ran while one was open for 0% of the time, Pallas kernels for 37%

profile of v2, /device:TPU:16, one launch (start us, length us, event | category | flops | bytes accessed | tf_op | source)
XLA Modules:
  0.0 80.2 jit_solution(10077238087679552174)
XLA Ops:
  0.0 0.1 shard_map.64
  0.1 1.3 %collective-permute-start = (bf16[64,4096]{1,0:T(8,128)(2,1)S(1)}, bf16[64,4096]{1,0:T(8,128)(2,1)S(1)}, u32[]{:S(2)}, u32[]{:S(2)}) collective-permute-start(bf16[64,4096]{1,0:T(8,128)(2,1)S(1)} %get-tuple-element.23.dep), channel_id=1, source_target_pairs={{0,1},{3,2},{4,5},{7,6},{8,9},{11,10},{12,13},{15,14},{16,17},{19,... | collective-permute-start | bytes 1572872 | tf_op jit(solution)/shard_map/ppermute | solution.py:485
  1.4 11.9 %shard_map.65 = (bf16[64,4096]{1,0:T(8,128)(2,1)S(1)}, bf16[64,4096]{1,0:T(8,128)(2,1)S(1)}, bf16[2,256,1024]{2,1,0:T(8,128)(2,1)S(1)}, bf16[2,64,4096]{2,1,0:T(...) custom-call(s32[8]{0:T(128)S(1)} %copy-done, ...), custom_call_target="tpu_custom_call", output_to_operand_aliasing={{4}: (6, {}), {5}: (7, {}), {6}: (8, {})} | custom-call | flops 1000 | bytes 1000 | tf_op jit(solution)/shard_map/pallas_call | solution.py:335
  13.4 1.5 %collective-permute-start.2 = (bf16[64,4096]{1,0:T(8,128)(2,1)S(1)}, bf16[64,4096]{1,0:T(8,128)(2,1)S(1)}, u32[]{:S(2)}, u32[]{:S(2)}) collective-permute-start(bf16[64,4096]{1,0:T(8,128)(2,1)S(1)} %get-tuple-element.30.refs_5_.left), channel_id=1, source_target_pairs={{0,1},{3,2},{4,5},{7,6},{8,9},{11,10},{12,13},{15,14},{16,17},{19,... | collective-permute-start | bytes 1572872 | tf_op jit(solution)/shard_map/ppermute | solution.py:485
  14.8 5.5 %shard_map.66 = (bf16[64,4096]{1,0:T(8,128)(2,1)S(1)}, bf16[64,4096]{1,0:T(8,128)(2,1)S(1)}) custom-call(s32[8]{0:T(128)S(1)} %copy-done, bf16[2,256,1024]{2,1,0:T(8,128)(2,1)S(1)} %get-tuple-element.24.refs_1_, bf16[2,2,256,256]{3,2,1,0:T(8,128)(2,1)S(1)} %get-tuple-element.25.refs_2_, bf16[2,1536,256]{2,1,0:T(8,128)(2,1)S(1)} %get-tuple-element.26.refs_3_, ...), custom_call_target="tpu_custom_call" | custom-call | flops 1000 | bytes 1000 | tf_op jit(solution)/shard_map/pallas_call | solution.py:373
  20.4 1.3 %collective-permute-start.4 = (bf16[64,4096]{1,0:T(8,128)(2,1)S(1)}, bf16[64,4096]{1,0:T(8,128)(2,1)S(1)}, u32[]{:S(2)}, u32[]{:S(2)}) collective-permute-start(bf16[64,4096]{1,0:T(8,128)(2,1)S(1)} %get-tuple-element.31.rest_0_.refs_2_), channel_id=1, source_target_pairs={{0,1},{3,2},{4,5},{7,6},{8,9},{11,10},{12,13},{15,14},{16,17},{19,... | collective-permute-start | bytes 1572872 | tf_op jit(solution)/shard_map/ppermute | solution.py:485
  21.7 0.0 collective-permute-done.right
  21.7 0.1 shard_map.67.refs_6_
  21.8 2.4 %collective-permute-start.3 = (bf16[64,4096]{1,0:T(8,128)(2,1)S(1)}, bf16[64,4096]{1,0:T(8,128)(2,1)S(1)}, u32[]{:S(2)}, u32[]{:S(2)}) collective-permute-start(bf16[64,4096]{1,0:T(8,128)(2,1)S(1)} %shard_map.67.refs_6_), channel_id=1, source_target_pairs={{1,2},{2,1},{5,6},{6,5},{9,10},{10,9},{13,14},{14,13},{17,18},{18,... | collective-permute-start | bytes 1572872 | tf_op jit(solution)/shard_map/ppermute | solution.py:485
  24.2 5.6 %shard_map.68.rest_0_.plain = bf16[2,64,4096]{2,1,0:T(8,128)(2,1)S(1)} custom-call(s32[8]{0:T(128)S(1)} %copy-done, bf16[2,256,1024]{2,1,0:T(8,128)(2,1)S(1)} %get-tuple-element.24.refs_1_, bf16[2,2,256,256]{3,2,1,0:T(8,128)(2,1)S(1)} %get-tuple-element.25.refs_2_, bf16[2,1536,256]{2,1,0:T(8,128)(2,1)S(1)} %get-tuple-element.26.refs_3_, ...), custom_call_target="tpu_custom_call" | custom-call | flops 4499999744 | bytes 1000 | tf_op jit(solution)/shard_map/pallas_call | solution.py:373
  29.8 1.9 %collective-permute-start.1 = (bf16[2,64,4096]{2,1,0:T(8,128)(2,1)S(1)}, bf16[2,64,4096]{2,1,0:T(8,128)(2,1)S(1)}, u32[]{:S(2)}, u32[]{:S(2)}) collective-permute-start(bf16[2,64,4096]{2,1,0:T(8,128)(2,1)S(1)} %shard_map.68.rest_0_.plain), channel_id=1, source_target_pairs={{1,5},{2,6},{5,9},{6,10},{9,13},{10,14},{13,17},{14,18},{17,21},{1... | collective-permute-start | bytes 3145736 | tf_op jit(solution)/shard_map/ppermute | solution.py:485
  31.7 1.2 %collective-permute-done.2.right = bf16[64,4096]{1,0:T(8,128)(2,1)S(1)} collective-permute-done((bf16[64,4096]{1,0:T(8,128)(2,1)S(1)}, bf16[64,4096]{1,0:T(8,128)(2,1)S(1)}, u32[]{:S(2)}, u32[]{:S(2)}) %collective-permute-start.2) | collective-permute-done | bytes 524320 | tf_op jit(solution)/shard_map/ppermute | solution.py:485
  32.9 0.1 shard_map.69.refs_5_
  33.0 2.3 %collective-permute-start.5 = (bf16[64,4096]{1,0:T(8,128)(2,1)S(1)}, bf16[64,4096]{1,0:T(8,128)(2,1)S(1)}, u32[]{:S(2)}, u32[]{:S(2)}) collective-permute-start(bf16[64,4096]{1,0:T(8,128)(2,1)S(1)} %shard_map.69.refs_5_), channel_id=1, source_target_pairs={{1,2},{2,1},{5,6},{6,5},{9,10},{10,9},{13,14},{14,13},{17,18},{18,... | collective-permute-start | bytes 1572872 | tf_op jit(solution)/shard_map/ppermute | solution.py:485
  35.3 1.5 %collective-permute-start.7 = (bf16[64,4096]{1,0:T(8,128)(2,1)S(1)}, bf16[64,4096]{1,0:T(8,128)(2,1)S(1)}, u32[]{:S(2)}, u32[]{:S(2)}) collective-permute-start(bf16[64,4096]{1,0:T(8,128)(2,1)S(1)} %get-tuple-element.34.refs_3_), channel_id=1, source_target_pairs={{0,1},{3,2},{4,5},{7,6},{8,9},{11,10},{12,13},{15,14},{16,17},{19,... | collective-permute-start | bytes 1572872 | tf_op jit(solution)/shard_map/ppermute | solution.py:485
  36.9 7.3 %collective-permute-done.4.refs_7_.right = bf16[64,4096]{1,0:T(8,128)(2,1)S(1)} collective-permute-done((bf16[64,4096]{1,0:T(8,128)(2,1)S(1)}, bf16[64,4096]{1,0:T(8,128)(2,1)S(1)}, u32[]{:S(2)}, u32[]{:S(2)}) %collective-permute-start.4) | collective-permute-done | bytes 524320 | tf_op jit(solution)/shard_map/ppermute | solution.py:485
  44.1 0.0 collective-permute-done.3.refs_6_.refs_4_
  44.1 5.5 %shard_map.70 = (bf16[64,4096]{1,0:T(8,128)(2,1)S(1)}, bf16[64,4096]{1,0:T(8,128)(2,1)S(1)}) custom-call(s32[8]{0:T(128)S(1)} %copy-done, bf16[2,256,1024]{2,1,0:T(8,128)(2,1)S(1)} %get-tuple-element.24.refs_1_, bf16[2,2,256,256]{3,2,1,0:T(8,128)(2,1)S(1)} %get-tuple-element.25.refs_2_, bf16[2,1536,256]{2,1,0:T(8,128)(2,1)S(1)} %get-tuple-element.26.refs_3_, ...), custom_call_target="tpu_custom_call" | custom-call | flops 1000 | bytes 1000 | tf_op jit(solution)/shard_map/pallas_call | solution.py:373
  49.7 0.0 collective-permute-done.5.refs_5_
  49.7 0.3 shard_map.71.rest_0_
  49.9 0.1 collective-permute-start.9
  50.0 0.1 shard_map.72
  50.2 0.2 collective-permute-start.6
  50.4 5.0 %collective-permute-done.7.right = bf16[64,4096]{1,0:T(8,128)(2,1)S(1)} collective-permute-done((bf16[64,4096]{1,0:T(8,128)(2,1)S(1)}, bf16[64,4096]{1,0:T(8,128)(2,1)S(1)}, u32[]{:S(2)}, u32[]{:S(2)}) %collective-permute-start.7) | collective-permute-done | bytes 524320 | tf_op jit(solution)/shard_map/ppermute | solution.py:485
  55.4 0.0 collective-permute-done.1.rest_1_.block
  55.4 0.1 shard_map.73
  55.5 0.1 collective-permute-start.8
  55.6 10.6 %collective-permute-done.6.refs_0_ = bf16[64,4096]{1,0:T(8,128)(2,1)S(1)} collective-permute-done((bf16[64,4096]{1,0:T(8,128)(2,1)S(1)}, bf16[64,4096]{1,0:T(8,128)(2,1)S(1)}, u32[]{:S(2)}, u32[]{:S(2)}) %collective-permute-start.6) | collective-permute-done | bytes 524320 | tf_op jit(solution)/shard_map/ppermute | solution.py:485
  66.1 11.1 %collective-permute-done.8.refs_1_ = bf16[64,4096]{1,0:T(8,128)(2,1)S(1)} collective-permute-done((bf16[64,4096]{1,0:T(8,128)(2,1)S(1)}, bf16[64,4096]{1,0:T(8,128)(2,1)S(1)}, u32[]{:S(2)}, u32[]{:S(2)}) %collective-permute-start.8) | collective-permute-done | bytes 524320 | tf_op jit(solution)/shard_map/ppermute | solution.py:485
  77.2 0.2 shard_map.74.wide
  77.4 1.2 %collective-permute-done.9.block = bf16[2,64,4096]{2,1,0:T(8,128)(2,1)S(1)} collective-permute-done((bf16[2,64,4096]{2,1,0:T(8,128)(2,1)S(1)}, bf16[2,64,4096]{2,1,0:T(8,128)(2,1)S(1)}, u32[]{:S(2)}, u32[]{:S(2)}) %collective-permute-start.9) | collective-permute-done | bytes 1048608 | tf_op jit(solution)/shard_map/ppermute | solution.py:485
  78.7 1.3 %shard_map.75 = bf16[64,2,4096]{2,1,0:T(2,128)(2,1)} custom-call(f32[2,64,4096]{2,1,0:T(8,128)S(1)} %shard_map.74.wide, bf16[2,64,4096]{2,1,0:T(8,128)(2,1)S(1)} %collective-permute-done.9.block), custom_call_target="tpu_custom_call" | custom-call | flops 1000 | bytes 1000 | tf_op jit(solution)/shard_map/pallas_call | solution.py:453
  (2 shorter events, 0.0 us)
Async XLA Ops:
  0.0 1.4 %copy-start = (s32[8]{0:T(128)S(1)}, s32[8]{0:T(128)}, u32[]{:S(2)}) copy-start(s32[8]{0:T(128)} %refs_0_.5) | copy-start | bytes 100
  0.1 21.6 %collective-permute-start = (bf16[64,4096]{1,0:T(8,128)(2,1)S(1)}, bf16[64,4096]{1,0:T(8,128)(2,1)S(1)}, u32[]{:S(2)}, u32[]{:S(2)}) collective-permute-start(bf16[64,4096]{1,0:T(8,128)(2,1)S(1)} %get-tuple-element.23.dep), channel_id=1, source_target_pairs={{0,1},{3,2},{4,5},{7,6},{8,9},{11,10},{12,13},{15,14},{16,17},{19,... | collective-permute-start | bytes 1572872 | tf_op jit(solution)/shard_map/ppermute | solution.py:485
  13.4 19.5 %collective-permute-start.2 = (bf16[64,4096]{1,0:T(8,128)(2,1)S(1)}, bf16[64,4096]{1,0:T(8,128)(2,1)S(1)}, u32[]{:S(2)}, u32[]{:S(2)}) collective-permute-start(bf16[64,4096]{1,0:T(8,128)(2,1)S(1)} %get-tuple-element.30.refs_5_.left), channel_id=1, source_target_pairs={{0,1},{3,2},{4,5},{7,6},{8,9},{11,10},{12,13},{15,14},{16,17},{19,... | collective-permute-start | bytes 1572872 | tf_op jit(solution)/shard_map/ppermute | solution.py:485
  20.4 23.7 %collective-permute-start.4 = (bf16[64,4096]{1,0:T(8,128)(2,1)S(1)}, bf16[64,4096]{1,0:T(8,128)(2,1)S(1)}, u32[]{:S(2)}, u32[]{:S(2)}) collective-permute-start(bf16[64,4096]{1,0:T(8,128)(2,1)S(1)} %get-tuple-element.31.rest_0_.refs_2_), channel_id=1, source_target_pairs={{0,1},{3,2},{4,5},{7,6},{8,9},{11,10},{12,13},{15,14},{16,17},{19,... | collective-permute-start | bytes 1572872 | tf_op jit(solution)/shard_map/ppermute | solution.py:485
  21.8 22.3 %collective-permute-start.3 = (bf16[64,4096]{1,0:T(8,128)(2,1)S(1)}, bf16[64,4096]{1,0:T(8,128)(2,1)S(1)}, u32[]{:S(2)}, u32[]{:S(2)}) collective-permute-start(bf16[64,4096]{1,0:T(8,128)(2,1)S(1)} %shard_map.67.refs_6_), channel_id=1, source_target_pairs={{1,2},{2,1},{5,6},{6,5},{9,10},{10,9},{13,14},{14,13},{17,18},{18,... | collective-permute-start | bytes 1572872 | tf_op jit(solution)/shard_map/ppermute | solution.py:485
  29.8 25.6 %collective-permute-start.1 = (bf16[2,64,4096]{2,1,0:T(8,128)(2,1)S(1)}, bf16[2,64,4096]{2,1,0:T(8,128)(2,1)S(1)}, u32[]{:S(2)}, u32[]{:S(2)}) collective-permute-start(bf16[2,64,4096]{2,1,0:T(8,128)(2,1)S(1)} %shard_map.68.rest_0_.plain), channel_id=1, source_target_pairs={{1,5},{2,6},{5,9},{6,10},{9,13},{10,14},{13,17},{14,18},{17,21},{1... | collective-permute-start | bytes 3145736 | tf_op jit(solution)/shard_map/ppermute | solution.py:485
  33.0 16.7 %collective-permute-start.5 = (bf16[64,4096]{1,0:T(8,128)(2,1)S(1)}, bf16[64,4096]{1,0:T(8,128)(2,1)S(1)}, u32[]{:S(2)}, u32[]{:S(2)}) collective-permute-start(bf16[64,4096]{1,0:T(8,128)(2,1)S(1)} %shard_map.69.refs_5_), channel_id=1, source_target_pairs={{1,2},{2,1},{5,6},{6,5},{9,10},{10,9},{13,14},{14,13},{17,18},{18,... | collective-permute-start | bytes 1572872 | tf_op jit(solution)/shard_map/ppermute | solution.py:485
  35.3 20.0 %collective-permute-start.7 = (bf16[64,4096]{1,0:T(8,128)(2,1)S(1)}, bf16[64,4096]{1,0:T(8,128)(2,1)S(1)}, u32[]{:S(2)}, u32[]{:S(2)}) collective-permute-start(bf16[64,4096]{1,0:T(8,128)(2,1)S(1)} %get-tuple-element.34.refs_3_), channel_id=1, source_target_pairs={{0,1},{3,2},{4,5},{7,6},{8,9},{11,10},{12,13},{15,14},{16,17},{19,... | collective-permute-start | bytes 1572872 | tf_op jit(solution)/shard_map/ppermute | solution.py:485
  49.9 28.7 %collective-permute-start.9 = (bf16[2,64,4096]{2,1,0:T(8,128)(2,1)S(1)}, bf16[2,64,4096]{2,1,0:T(8,128)(2,1)S(1)}, u32[]{:S(2)}, u32[]{:S(2)}) collective-permute-start(bf16[2,64,4096]{2,1,0:T(8,128)(2,1)S(1)} %shard_map.71.rest_0_), channel_id=1, source_target_pairs={{0,5},{3,6},{1,4},{2,7},{4,9},{7,10},{5,8},{6,11},{8,13},{11,14},{... | collective-permute-start | bytes 3145736 | tf_op jit(solution)/shard_map/ppermute | solution.py:485
  50.2 16.0 %collective-permute-start.6 = (bf16[64,4096]{1,0:T(8,128)(2,1)S(1)}, bf16[64,4096]{1,0:T(8,128)(2,1)S(1)}, u32[]{:S(2)}, u32[]{:S(2)}) collective-permute-start(bf16[64,4096]{1,0:T(8,128)(2,1)S(1)} %shard_map.72), channel_id=1, source_target_pairs={{1,6},{2,5},{0,4},{3,7},{5,10},{6,9},{4,8},{7,11},{9,14},{10,13},{... | collective-permute-start | bytes 1572872 | tf_op jit(solution)/shard_map/ppermute | solution.py:485
  55.5 21.7 %collective-permute-start.8 = (bf16[64,4096]{1,0:T(8,128)(2,1)S(1)}, bf16[64,4096]{1,0:T(8,128)(2,1)S(1)}, u32[]{:S(2)}, u32[]{:S(2)}) collective-permute-start(bf16[64,4096]{1,0:T(8,128)(2,1)S(1)} %shard_map.73), channel_id=1, source_target_pairs={{1,6},{2,5},{0,4},{3,7},{5,10},{6,9},{4,8},{7,11},{9,14},{10,13},{... | collective-permute-start | bytes 1572872 | tf_op jit(solution)/shard_map/ppermute | solution.py:485

commit v3 on v2

--- a/solution.py
+++ b/solution.py
@@ -13,7 +13,7 @@
 HD = 128
 GROUP = QH // KVH
 KEY_BLOCK = 512
-WEIGHT_PARTS = 4
+WEIGHT_PARTS = 2
 COLUMN_TILE = 1024
 
 neg_large = -1e30
@@ -162,7 +162,7 @@
                     sem.at[used + 1 + index],
                 )
             )
-        early = len(w_copies) // 2
+        early = len(w_copies)
         for copy in copies + w_copies[:early]:
             copy.start()
         for copy in copies:

time: 80.4 us -> 79.5 us (0.989)
  Pallas kernels: 31 us -> 29 us
  waiting for transfers between devices: 36.4 us -> 38 us
    pallas_call x1, Pallas kernels: 11.9 us -> 9.92 us  [second_rows(): pl.pallas_call(functools.partial(second_kernel, ticks, rows, choose, acti...]
    ppermute x10, waiting for transfers between devices: 36.4 us -> 38 us  [send(): return lax.ppermute(block, ('section', 'head'), route)]
  transfers between devices with their start and end apart: 10 -> 10, of which waited for: 6 -> 7; matrix products, arithmetic and copies ran while one was open for 0% -> 0% of each run, Pallas kernels for 37% -> 35%
where the time goes in v3:
time: 79.5 us; the launch traced here: 79.3 us
  waiting for transfers between devices  38 us (48%)
  Pallas kernels  29 us (36%)
  starting transfers between devices  12 us (15%)
    ppermute x10, waiting for transfers between devices, send(): return lax.ppermute(block, ('section', 'head'), route)  38 us
    pallas_call x3, Pallas kernels, project_rows(): pl.pallas_call(functools.partial(rows_kernel, ticks, rows, choose, names)...  16.7 us
    ppermute x10, starting transfers between devices, send(): return lax.ppermute(block, ('section', 'head'), route)  12 us
    pallas_call x1, Pallas kernels, second_rows(): pl.pallas_call(functools.partial(second_kernel, ticks, rows, choose, acti...  9.92 us
  transfers between devices with their start and end apart: 10, of which 7 were waited for; matrix products, arithmetic and copies ran while one was open for 0% of the time, Pallas kernels for 35%

profile of v3, /device:TPU:16, one launch (start us, length us, event | category | flops | bytes accessed | tf_op | source)
XLA Modules:
  0.0 79.3 jit_solution(1662489931262692164)
XLA Ops:
  0.0 0.1 shard_map.64
  0.1 1.3 %collective-permute-start = (bf16[64,4096]{1,0:T(8,128)(2,1)S(1)}, bf16[64,4096]{1,0:T(8,128)(2,1)S(1)}, u32[]{:S(2)}, u32[]{:S(2)}) collective-permute-start(bf16[64,4096]{1,0:T(8,128)(2,1)S(1)} %get-tuple-element.23.dep), channel_id=1, source_target_pairs={{0,1},{3,2},{4,5},{7,6},{8,9},{11,10},{12,13},{15,14},{16,17},{19,... | collective-permute-start | bytes 1572872 | tf_op jit(solution)/shard_map/ppermute | solution.py:485
  1.4 9.9 %shard_map.65 = (bf16[64,4096]{1,0:T(8,128)(2,1)S(1)}, bf16[64,4096]{1,0:T(8,128)(2,1)S(1)}, bf16[2,256,1024]{2,1,0:T(8,128)(2,1)S(1)}, bf16[2,64,4096]{2,1,0:T(...) custom-call(s32[8]{0:T(128)S(1)} %copy-done, ...), custom_call_target="tpu_custom_call", output_to_operand_aliasing={{4}: (6, {}), {5}: (7, {}), {6}: (8, {})} | custom-call | flops 1000 | bytes 1000 | tf_op jit(solution)/shard_map/pallas_call | solution.py:335
  11.3 1.5 %collective-permute-start.2 = (bf16[64,4096]{1,0:T(8,128)(2,1)S(1)}, bf16[64,4096]{1,0:T(8,128)(2,1)S(1)}, u32[]{:S(2)}, u32[]{:S(2)}) collective-permute-start(bf16[64,4096]{1,0:T(8,128)(2,1)S(1)} %get-tuple-element.30.refs_5_.left), channel_id=1, source_target_pairs={{0,1},{3,2},{4,5},{7,6},{8,9},{11,10},{12,13},{15,14},{16,17},{19,... | collective-permute-start | bytes 1572872 | tf_op jit(solution)/shard_map/ppermute | solution.py:485
  12.8 5.5 %shard_map.66 = (bf16[64,4096]{1,0:T(8,128)(2,1)S(1)}, bf16[64,4096]{1,0:T(8,128)(2,1)S(1)}) custom-call(s32[8]{0:T(128)S(1)} %copy-done, bf16[2,256,1024]{2,1,0:T(8,128)(2,1)S(1)} %get-tuple-element.24.refs_1_, bf16[2,2,256,256]{3,2,1,0:T(8,128)(2,1)S(1)} %get-tuple-element.25.refs_2_, bf16[2,1536,256]{2,1,0:T(8,128)(2,1)S(1)} %get-tuple-element.26.refs_3_, ...), custom_call_target="tpu_custom_call" | custom-call | flops 1000 | bytes 1000 | tf_op jit(solution)/shard_map/pallas_call | solution.py:373
  18.4 1.3 %collective-permute-start.4 = (bf16[64,4096]{1,0:T(8,128)(2,1)S(1)}, bf16[64,4096]{1,0:T(8,128)(2,1)S(1)}, u32[]{:S(2)}, u32[]{:S(2)}) collective-permute-start(bf16[64,4096]{1,0:T(8,128)(2,1)S(1)} %get-tuple-element.31.rest_0_.refs_2_), channel_id=1, source_target_pairs={{0,1},{3,2},{4,5},{7,6},{8,9},{11,10},{12,13},{15,14},{16,17},{19,... | collective-permute-start | bytes 1572872 | tf_op jit(solution)/shard_map/ppermute | solution.py:485
  19.7 1.1 %collective-permute-done.right = bf16[64,4096]{1,0:T(8,128)(2,1)S(1)} collective-permute-done((bf16[64,4096]{1,0:T(8,128)(2,1)S(1)}, bf16[64,4096]{1,0:T(8,128)(2,1)S(1)}, u32[]{:S(2)}, u32[]{:S(2)}) %collective-permute-start) | collective-permute-done | bytes 524320 | tf_op jit(solution)/shard_map/ppermute | solution.py:485
  20.8 0.1 shard_map.67.refs_6_
  20.9 1.9 %collective-permute-start.3 = (bf16[64,4096]{1,0:T(8,128)(2,1)S(1)}, bf16[64,4096]{1,0:T(8,128)(2,1)S(1)}, u32[]{:S(2)}, u32[]{:S(2)}) collective-permute-start(bf16[64,4096]{1,0:T(8,128)(2,1)S(1)} %shard_map.67.refs_6_), channel_id=1, source_target_pairs={{1,2},{2,1},{5,6},{6,5},{9,10},{10,9},{13,14},{14,13},{17,18},{18,... | collective-permute-start | bytes 1572872 | tf_op jit(solution)/shard_map/ppermute | solution.py:485
  22.8 5.6 %shard_map.68.rest_0_.plain = bf16[2,64,4096]{2,1,0:T(8,128)(2,1)S(1)} custom-call(s32[8]{0:T(128)S(1)} %copy-done, bf16[2,256,1024]{2,1,0:T(8,128)(2,1)S(1)} %get-tuple-element.24.refs_1_, bf16[2,2,256,256]{3,2,1,0:T(8,128)(2,1)S(1)} %get-tuple-element.25.refs_2_, bf16[2,1536,256]{2,1,0:T(8,128)(2,1)S(1)} %get-tuple-element.26.refs_3_, ...), custom_call_target="tpu_custom_call" | custom-call | flops 4499999744 | bytes 1000 | tf_op jit(solution)/shard_map/pallas_call | solution.py:373
  28.4 1.9 %collective-permute-start.1 = (bf16[2,64,4096]{2,1,0:T(8,128)(2,1)S(1)}, bf16[2,64,4096]{2,1,0:T(8,128)(2,1)S(1)}, u32[]{:S(2)}, u32[]{:S(2)}) collective-permute-start(bf16[2,64,4096]{2,1,0:T(8,128)(2,1)S(1)} %shard_map.68.rest_0_.plain), channel_id=1, source_target_pairs={{1,5},{2,6},{5,9},{6,10},{9,13},{10,14},{13,17},{14,18},{17,21},{1... | collective-permute-start | bytes 3145736 | tf_op jit(solution)/shard_map/ppermute | solution.py:485
  30.4 1.7 %collective-permute-done.2.right = bf16[64,4096]{1,0:T(8,128)(2,1)S(1)} collective-permute-done((bf16[64,4096]{1,0:T(8,128)(2,1)S(1)}, bf16[64,4096]{1,0:T(8,128)(2,1)S(1)}, u32[]{:S(2)}, u32[]{:S(2)}) %collective-permute-start.2) | collective-permute-done | bytes 524320 | tf_op jit(solution)/shard_map/ppermute | solution.py:485
  32.0 0.1 shard_map.69.refs_5_
  32.1 2.3 %collective-permute-start.5 = (bf16[64,4096]{1,0:T(8,128)(2,1)S(1)}, bf16[64,4096]{1,0:T(8,128)(2,1)S(1)}, u32[]{:S(2)}, u32[]{:S(2)}) collective-permute-start(bf16[64,4096]{1,0:T(8,128)(2,1)S(1)} %shard_map.69.refs_5_), channel_id=1, source_target_pairs={{1,2},{2,1},{5,6},{6,5},{9,10},{10,9},{13,14},{14,13},{17,18},{18,... | collective-permute-start | bytes 1572872 | tf_op jit(solution)/shard_map/ppermute | solution.py:485
  34.4 1.5 %collective-permute-start.7 = (bf16[64,4096]{1,0:T(8,128)(2,1)S(1)}, bf16[64,4096]{1,0:T(8,128)(2,1)S(1)}, u32[]{:S(2)}, u32[]{:S(2)}) collective-permute-start(bf16[64,4096]{1,0:T(8,128)(2,1)S(1)} %get-tuple-element.34.refs_3_), channel_id=1, source_target_pairs={{0,1},{3,2},{4,5},{7,6},{8,9},{11,10},{12,13},{15,14},{16,17},{19,... | collective-permute-start | bytes 1572872 | tf_op jit(solution)/shard_map/ppermute | solution.py:485
  35.9 7.3 %collective-permute-done.4.refs_7_.right = bf16[64,4096]{1,0:T(8,128)(2,1)S(1)} collective-permute-done((bf16[64,4096]{1,0:T(8,128)(2,1)S(1)}, bf16[64,4096]{1,0:T(8,128)(2,1)S(1)}, u32[]{:S(2)}, u32[]{:S(2)}) %collective-permute-start.4) | collective-permute-done | bytes 524320 | tf_op jit(solution)/shard_map/ppermute | solution.py:485
  43.2 0.0 collective-permute-done.3.refs_6_.refs_4_
  43.2 5.5 %shard_map.70 = (bf16[64,4096]{1,0:T(8,128)(2,1)S(1)}, bf16[64,4096]{1,0:T(8,128)(2,1)S(1)}) custom-call(s32[8]{0:T(128)S(1)} %copy-done, bf16[2,256,1024]{2,1,0:T(8,128)(2,1)S(1)} %get-tuple-element.24.refs_1_, bf16[2,2,256,256]{3,2,1,0:T(8,128)(2,1)S(1)} %get-tuple-element.25.refs_2_, bf16[2,1536,256]{2,1,0:T(8,128)(2,1)S(1)} %get-tuple-element.26.refs_3_, ...), custom_call_target="tpu_custom_call" | custom-call | flops 1000 | bytes 1000 | tf_op jit(solution)/shard_map/pallas_call | solution.py:373
  48.8 0.0 collective-permute-done.5.refs_5_
  48.8 0.3 shard_map.71.rest_0_
  49.1 0.1 collective-permute-start.9
  49.1 0.1 shard_map.72
  49.3 0.2 collective-permute-start.6
  49.4 5.1 %collective-permute-done.7.right = bf16[64,4096]{1,0:T(8,128)(2,1)S(1)} collective-permute-done((bf16[64,4096]{1,0:T(8,128)(2,1)S(1)}, bf16[64,4096]{1,0:T(8,128)(2,1)S(1)}, u32[]{:S(2)}, u32[]{:S(2)}) %collective-permute-start.7) | collective-permute-done | bytes 524320 | tf_op jit(solution)/shard_map/ppermute | solution.py:485
  54.5 0.0 collective-permute-done.1.rest_1_.block
  54.5 0.1 shard_map.73
  54.6 0.1 collective-permute-start.8
  54.7 10.6 %collective-permute-done.6.refs_0_ = bf16[64,4096]{1,0:T(8,128)(2,1)S(1)} collective-permute-done((bf16[64,4096]{1,0:T(8,128)(2,1)S(1)}, bf16[64,4096]{1,0:T(8,128)(2,1)S(1)}, u32[]{:S(2)}, u32[]{:S(2)}) %collective-permute-start.6) | collective-permute-done | bytes 524320 | tf_op jit(solution)/shard_map/ppermute | solution.py:485
  65.3 11.1 %collective-permute-done.8.refs_1_ = bf16[64,4096]{1,0:T(8,128)(2,1)S(1)} collective-permute-done((bf16[64,4096]{1,0:T(8,128)(2,1)S(1)}, bf16[64,4096]{1,0:T(8,128)(2,1)S(1)}, u32[]{:S(2)}, u32[]{:S(2)}) %collective-permute-start.8) | collective-permute-done | bytes 524320 | tf_op jit(solution)/shard_map/ppermute | solution.py:485
  76.4 0.2 shard_map.74.wide
  76.6 1.2 %collective-permute-done.9.block = bf16[2,64,4096]{2,1,0:T(8,128)(2,1)S(1)} collective-permute-done((bf16[2,64,4096]{2,1,0:T(8,128)(2,1)S(1)}, bf16[2,64,4096]{2,1,0:T(8,128)(2,1)S(1)}, u32[]{:S(2)}, u32[]{:S(2)}) %collective-permute-start.9) | collective-permute-done | bytes 1048608 | tf_op jit(solution)/shard_map/ppermute | solution.py:485
  77.7 1.3 %shard_map.75 = bf16[64,2,4096]{2,1,0:T(2,128)(2,1)} custom-call(f32[2,64,4096]{2,1,0:T(8,128)S(1)} %shard_map.74.wide, bf16[2,64,4096]{2,1,0:T(8,128)(2,1)S(1)} %collective-permute-done.9.block), custom_call_target="tpu_custom_call" | custom-call | flops 1000 | bytes 1000 | tf_op jit(solution)/shard_map/pallas_call | solution.py:453
  (2 shorter events, 0.0 us)
Async XLA Ops:
  0.0 1.4 %copy-start = (s32[8]{0:T(128)S(1)}, s32[8]{0:T(128)}, u32[]{:S(2)}) copy-start(s32[8]{0:T(128)} %refs_0_.5) | copy-start | bytes 100
  0.1 20.7 %collective-permute-start = (bf16[64,4096]{1,0:T(8,128)(2,1)S(1)}, bf16[64,4096]{1,0:T(8,128)(2,1)S(1)}, u32[]{:S(2)}, u32[]{:S(2)}) collective-permute-start(bf16[64,4096]{1,0:T(8,128)(2,1)S(1)} %get-tuple-element.23.dep), channel_id=1, source_target_pairs={{0,1},{3,2},{4,5},{7,6},{8,9},{11,10},{12,13},{15,14},{16,17},{19,... | collective-permute-start | bytes 1572872 | tf_op jit(solution)/shard_map/ppermute | solution.py:485
  11.3 20.7 %collective-permute-start.2 = (bf16[64,4096]{1,0:T(8,128)(2,1)S(1)}, bf16[64,4096]{1,0:T(8,128)(2,1)S(1)}, u32[]{:S(2)}, u32[]{:S(2)}) collective-permute-start(bf16[64,4096]{1,0:T(8,128)(2,1)S(1)} %get-tuple-element.30.refs_5_.left), channel_id=1, source_target_pairs={{0,1},{3,2},{4,5},{7,6},{8,9},{11,10},{12,13},{15,14},{16,17},{19,... | collective-permute-start | bytes 1572872 | tf_op jit(solution)/shard_map/ppermute | solution.py:485
  18.4 24.9 %collective-permute-start.4 = (bf16[64,4096]{1,0:T(8,128)(2,1)S(1)}, bf16[64,4096]{1,0:T(8,128)(2,1)S(1)}, u32[]{:S(2)}, u32[]{:S(2)}) collective-permute-start(bf16[64,4096]{1,0:T(8,128)(2,1)S(1)} %get-tuple-element.31.rest_0_.refs_2_), channel_id=1, source_target_pairs={{0,1},{3,2},{4,5},{7,6},{8,9},{11,10},{12,13},{15,14},{16,17},{19,... | collective-permute-start | bytes 1572872 | tf_op jit(solution)/shard_map/ppermute | solution.py:485
  20.9 22.3 %collective-permute-start.3 = (bf16[64,4096]{1,0:T(8,128)(2,1)S(1)}, bf16[64,4096]{1,0:T(8,128)(2,1)S(1)}, u32[]{:S(2)}, u32[]{:S(2)}) collective-permute-start(bf16[64,4096]{1,0:T(8,128)(2,1)S(1)} %shard_map.67.refs_6_), channel_id=1, source_target_pairs={{1,2},{2,1},{5,6},{6,5},{9,10},{10,9},{13,14},{14,13},{17,18},{18,... | collective-permute-start | bytes 1572872 | tf_op jit(solution)/shard_map/ppermute | solution.py:485
  28.4 26.1 %collective-permute-start.1 = (bf16[2,64,4096]{2,1,0:T(8,128)(2,1)S(1)}, bf16[2,64,4096]{2,1,0:T(8,128)(2,1)S(1)}, u32[]{:S(2)}, u32[]{:S(2)}) collective-permute-start(bf16[2,64,4096]{2,1,0:T(8,128)(2,1)S(1)} %shard_map.68.rest_0_.plain), channel_id=1, source_target_pairs={{1,5},{2,6},{5,9},{6,10},{9,13},{10,14},{13,17},{14,18},{17,21},{1... | collective-permute-start | bytes 3145736 | tf_op jit(solution)/shard_map/ppermute | solution.py:485
  32.1 16.7 %collective-permute-start.5 = (bf16[64,4096]{1,0:T(8,128)(2,1)S(1)}, bf16[64,4096]{1,0:T(8,128)(2,1)S(1)}, u32[]{:S(2)}, u32[]{:S(2)}) collective-permute-start(bf16[64,4096]{1,0:T(8,128)(2,1)S(1)} %shard_map.69.refs_5_), channel_id=1, source_target_pairs={{1,2},{2,1},{5,6},{6,5},{9,10},{10,9},{13,14},{14,13},{17,18},{18,... | collective-permute-start | bytes 1572872 | tf_op jit(solution)/shard_map/ppermute | solution.py:485
  34.4 20.1 %collective-permute-start.7 = (bf16[64,4096]{1,0:T(8,128)(2,1)S(1)}, bf16[64,4096]{1,0:T(8,128)(2,1)S(1)}, u32[]{:S(2)}, u32[]{:S(2)}) collective-permute-start(bf16[64,4096]{1,0:T(8,128)(2,1)S(1)} %get-tuple-element.34.refs_3_), channel_id=1, source_target_pairs={{0,1},{3,2},{4,5},{7,6},{8,9},{11,10},{12,13},{15,14},{16,17},{19,... | collective-permute-start | bytes 1572872 | tf_op jit(solution)/shard_map/ppermute | solution.py:485
  49.1 28.7 %collective-permute-start.9 = (bf16[2,64,4096]{2,1,0:T(8,128)(2,1)S(1)}, bf16[2,64,4096]{2,1,0:T(8,128)(2,1)S(1)}, u32[]{:S(2)}, u32[]{:S(2)}) collective-permute-start(bf16[2,64,4096]{2,1,0:T(8,128)(2,1)S(1)} %shard_map.71.rest_0_), channel_id=1, source_target_pairs={{0,5},{3,6},{1,4},{2,7},{4,9},{7,10},{5,8},{6,11},{8,13},{11,14},{... | collective-permute-start | bytes 3145736 | tf_op jit(solution)/shard_map/ppermute | solution.py:485
  49.3 16.0 %collective-permute-start.6 = (bf16[64,4096]{1,0:T(8,128)(2,1)S(1)}, bf16[64,4096]{1,0:T(8,128)(2,1)S(1)}, u32[]{:S(2)}, u32[]{:S(2)}) collective-permute-start(bf16[64,4096]{1,0:T(8,128)(2,1)S(1)} %shard_map.72), channel_id=1, source_target_pairs={{1,6},{2,5},{0,4},{3,7},{5,10},{6,9},{4,8},{7,11},{9,14},{10,13},{... | collective-permute-start | bytes 1572872 | tf_op jit(solution)/shard_map/ppermute | solution.py:485
  54.6 21.8 %collective-permute-start.8 = (bf16[64,4096]{1,0:T(8,128)(2,1)S(1)}, bf16[64,4096]{1,0:T(8,128)(2,1)S(1)}, u32[]{:S(2)}, u32[]{:S(2)}) collective-permute-start(bf16[64,4096]{1,0:T(8,128)(2,1)S(1)} %shard_map.73), channel_id=1, source_target_pairs={{1,6},{2,5},{0,4},{3,7},{5,10},{6,9},{4,8},{7,11},{9,14},{10,13},{... | collective-permute-start | bytes 1572872 | tf_op jit(solution)/shard_map/ppermute | solution.py:485

commit v4 on v3

--- a/solution.py
+++ b/solution.py
@@ -96,25 +96,12 @@
             out[:, here] = product[index * rows : (index + 1) * rows].astype(out.dtype)
 
 
-def project_arriving(heads_ref, w_ref, outs, sum_ref, copies):
-    rows, columns = outs[0].shape
-    tile = min(COLUMN_TILE, columns)
-    part_rows = w_ref.shape[0] // len(copies)
+def project_arriving(heads_ref, w_ref, outs, copies):
+    part_columns = w_ref.shape[1] // len(copies)
     for part, copy in enumerate(copies):
         copy.wait()
-        depth = slice(part * part_rows, (part + 1) * part_rows)
-        for first in range(0, columns, tile):
-            here = slice(first, first + tile)
-            product = jnp.dot(
-                heads_ref[:, depth], w_ref[depth, here], preferred_element_type=jnp.float32
-            )
-            if part > 0:
-                product = product + sum_ref[:, here]
-            if part < len(copies) - 1:
-                sum_ref[:, here] = product
-            else:
-                for index, out in enumerate(outs):
-                    out[:, here] = product[index * rows : (index + 1) * rows].astype(out.dtype)
+        here = pl.ds(part * part_columns, part_columns)
+        project(heads_ref, w_ref.at[:, here], [out.at[:, here] for out in outs])
 
 
 def held_copies(new_kv, cache_kv, out_weight, fresh_ref, cache_ref, w_ref, sem):
@@ -128,10 +115,10 @@
             pairs.append((new_kv.at[tick, part, :, lanes], fresh_ref.at[tick, part]))
     for part in range(2):
         pairs.append((cache_kv.at[part, :, lanes], cache_ref.at[part]))
-    part_rows = w_ref.shape[0] // WEIGHT_PARTS
+    part_columns = w_ref.shape[1] // WEIGHT_PARTS
     for part in range(WEIGHT_PARTS):
-        here = pl.ds(part * part_rows, part_rows)
-        pairs.append((out_weight.at[0, here, :], w_ref.at[here, :]))
+        here = pl.ds(part * part_columns, part_columns)
+        pairs.append((out_weight.at[0, :, here], w_ref.at[:, here]))
     copies = [
         pltpu.make_async_copy(source, target, sem.at[index])
         for index, (source, target) in enumerate(pairs)
@@ -143,7 +130,7 @@
     ticks, rows, choose, active, lengths, queries, new_kv, cache_kv, out_weight, *rest
 ):
     outs = rest[: len(ticks)]
-    fresh_ref, cache_ref, w_ref, length_ref, q_ref, heads_ref, sum_ref, sem = rest[len(ticks) :]
+    fresh_ref, cache_ref, w_ref, length_ref, q_ref, heads_ref, sem = rest[len(ticks) :]
     z = lax.axis_index("head")
 
     @pl.when(active(z))
@@ -162,13 +149,10 @@
                     sem.at[used + 1 + index],
                 )
             )
-        early = len(w_copies)
-        for copy in copies + w_copies[:early]:
+        for copy in copies[::-1] + w_copies:
             copy.start()
         for copy in copies:
             copy.wait()
-        for copy in w_copies[early:]:
-            copy.start()
         attend(
             ticks,
             rows,
@@ -179,7 +163,7 @@
             cache_ref,
             heads_ref,
         )
-        project_arriving(heads_ref, w_ref, outs, sum_ref, w_copies)
+        project_arriving(heads_ref, w_ref, outs, w_copies)
 
 
 def later_rows(ticks, rows, choose, lengths, q_ref, fresh_ref, cache_ref, heads_ref):
@@ -314,7 +298,6 @@
             pltpu.SMEM(lengths.shape, lengths.dtype),
             pltpu.VMEM((len(ticks), rows, head_width), kind),
             pltpu.VMEM((len(ticks) * rows, head_width), kind),
-            pltpu.VMEM((len(ticks) * rows, columns), jnp.float32),
             pltpu.SemaphoreType.DMA((3 + 2 * tick_count + WEIGHT_PARTS + len(ticks),)),
         ],
         compiler_params=PARAMS,

time: 79.5 us -> 79.3 us (level)
  no operation moved by 1% of the time
where the time goes in v4:
time: 79.3 us; the launch traced here: 79.1 us
  waiting for transfers between devices  37.8 us (48%)
  Pallas kernels  29 us (37%)
  starting transfers between devices  12 us (15%)
    ppermute x10, waiting for transfers between devices, send(): return lax.ppermute(block, ('section', 'head'), route)  37.8 us
    pallas_call x3, Pallas kernels, project_rows(): pl.pallas_call(functools.partial(rows_kernel, ticks, rows, choose, names)...  16.7 us
    ppermute x10, starting transfers between devices, send(): return lax.ppermute(block, ('section', 'head'), route)  12 us
    pallas_call x1, Pallas kernels, second_rows(): pl.pallas_call(functools.partial(second_kernel, ticks, rows, choose, acti...  9.92 us
  transfers between devices with their start and end apart: 10, of which 7 were waited for; matrix products, arithmetic and copies ran while one was open for 0% of the time, Pallas kernels for 35%

profile of v4, /device:TPU:16, one launch (start us, length us, event | category | flops | bytes accessed | tf_op | source)
XLA Modules:
  0.0 79.1 jit_solution(1820863546743308382)
XLA Ops:
  0.0 0.1 shard_map.64
  0.1 1.3 %collective-permute-start = (bf16[64,4096]{1,0:T(8,128)(2,1)S(1)}, bf16[64,4096]{1,0:T(8,128)(2,1)S(1)}, u32[]{:S(2)}, u32[]{:S(2)}) collective-permute-start(bf16[64,4096]{1,0:T(8,128)(2,1)S(1)} %get-tuple-element.23.dep), channel_id=1, source_target_pairs={{0,1},{3,2},{4,5},{7,6},{8,9},{11,10},{12,13},{15,14},{16,17},{19,... | collective-permute-start | bytes 1572872 | tf_op jit(solution)/shard_map/ppermute | solution.py:468
  1.4 9.9 %shard_map.65 = (bf16[64,4096]{1,0:T(8,128)(2,1)S(1)}, bf16[64,4096]{1,0:T(8,128)(2,1)S(1)}, bf16[2,256,1024]{2,1,0:T(8,128)(2,1)S(1)}, bf16[2,64,4096]{2,1,0:T(...) custom-call(s32[8]{0:T(128)S(1)} %copy-done, ...), custom_call_target="tpu_custom_call", output_to_operand_aliasing={{4}: (6, {}), {5}: (7, {}), {6}: (8, {})} | custom-call | flops 1000 | bytes 1000 | tf_op jit(solution)/shard_map/pallas_call | solution.py:318
  11.3 1.5 %collective-permute-start.2 = (bf16[64,4096]{1,0:T(8,128)(2,1)S(1)}, bf16[64,4096]{1,0:T(8,128)(2,1)S(1)}, u32[]{:S(2)}, u32[]{:S(2)}) collective-permute-start(bf16[64,4096]{1,0:T(8,128)(2,1)S(1)} %get-tuple-element.30.refs_5_.left), channel_id=1, source_target_pairs={{0,1},{3,2},{4,5},{7,6},{8,9},{11,10},{12,13},{15,14},{16,17},{19,... | collective-permute-start | bytes 1572872 | tf_op jit(solution)/shard_map/ppermute | solution.py:468
  12.8 5.5 %shard_map.66 = (bf16[64,4096]{1,0:T(8,128)(2,1)S(1)}, bf16[64,4096]{1,0:T(8,128)(2,1)S(1)}) custom-call(s32[8]{0:T(128)S(1)} %copy-done, bf16[2,256,1024]{2,1,0:T(8,128)(2,1)S(1)} %get-tuple-element.24.refs_1_, bf16[2,2,256,256]{3,2,1,0:T(8,128)(2,1)S(1)} %get-tuple-element.25.refs_2_, bf16[2,1536,256]{2,1,0:T(8,128)(2,1)S(1)} %get-tuple-element.26.refs_3_, ...), custom_call_target="tpu_custom_call" | custom-call | flops 1000 | bytes 1000 | tf_op jit(solution)/shard_map/pallas_call | solution.py:356
  18.4 1.3 %collective-permute-start.4 = (bf16[64,4096]{1,0:T(8,128)(2,1)S(1)}, bf16[64,4096]{1,0:T(8,128)(2,1)S(1)}, u32[]{:S(2)}, u32[]{:S(2)}) collective-permute-start(bf16[64,4096]{1,0:T(8,128)(2,1)S(1)} %get-tuple-element.31.rest_0_.refs_2_), channel_id=1, source_target_pairs={{0,1},{3,2},{4,5},{7,6},{8,9},{11,10},{12,13},{15,14},{16,17},{19,... | collective-permute-start | bytes 1572872 | tf_op jit(solution)/shard_map/ppermute | solution.py:468
  19.7 0.9 %collective-permute-done.right = bf16[64,4096]{1,0:T(8,128)(2,1)S(1)} collective-permute-done((bf16[64,4096]{1,0:T(8,128)(2,1)S(1)}, bf16[64,4096]{1,0:T(8,128)(2,1)S(1)}, u32[]{:S(2)}, u32[]{:S(2)}) %collective-permute-start) | collective-permute-done | bytes 524320 | tf_op jit(solution)/shard_map/ppermute | solution.py:468
  20.6 0.1 shard_map.67.refs_6_
  20.7 1.9 %collective-permute-start.3 = (bf16[64,4096]{1,0:T(8,128)(2,1)S(1)}, bf16[64,4096]{1,0:T(8,128)(2,1)S(1)}, u32[]{:S(2)}, u32[]{:S(2)}) collective-permute-start(bf16[64,4096]{1,0:T(8,128)(2,1)S(1)} %shard_map.67.refs_6_), channel_id=1, source_target_pairs={{1,2},{2,1},{5,6},{6,5},{9,10},{10,9},{13,14},{14,13},{17,18},{18,... | collective-permute-start | bytes 1572872 | tf_op jit(solution)/shard_map/ppermute | solution.py:468
  22.6 5.6 %shard_map.68.rest_0_.plain = bf16[2,64,4096]{2,1,0:T(8,128)(2,1)S(1)} custom-call(s32[8]{0:T(128)S(1)} %copy-done, bf16[2,256,1024]{2,1,0:T(8,128)(2,1)S(1)} %get-tuple-element.24.refs_1_, bf16[2,2,256,256]{3,2,1,0:T(8,128)(2,1)S(1)} %get-tuple-element.25.refs_2_, bf16[2,1536,256]{2,1,0:T(8,128)(2,1)S(1)} %get-tuple-element.26.refs_3_, ...), custom_call_target="tpu_custom_call" | custom-call | flops 4499999744 | bytes 1000 | tf_op jit(solution)/shard_map/pallas_call | solution.py:356
  28.2 1.9 %collective-permute-start.1 = (bf16[2,64,4096]{2,1,0:T(8,128)(2,1)S(1)}, bf16[2,64,4096]{2,1,0:T(8,128)(2,1)S(1)}, u32[]{:S(2)}, u32[]{:S(2)}) collective-permute-start(bf16[2,64,4096]{2,1,0:T(8,128)(2,1)S(1)} %shard_map.68.rest_0_.plain), channel_id=1, source_target_pairs={{1,5},{2,6},{5,9},{6,10},{9,13},{10,14},{13,17},{14,18},{17,21},{1... | collective-permute-start | bytes 3145736 | tf_op jit(solution)/shard_map/ppermute | solution.py:468
  30.2 1.7 %collective-permute-done.2.right = bf16[64,4096]{1,0:T(8,128)(2,1)S(1)} collective-permute-done((bf16[64,4096]{1,0:T(8,128)(2,1)S(1)}, bf16[64,4096]{1,0:T(8,128)(2,1)S(1)}, u32[]{:S(2)}, u32[]{:S(2)}) %collective-permute-start.2) | collective-permute-done | bytes 524320 | tf_op jit(solution)/shard_map/ppermute | solution.py:468
  31.8 0.1 shard_map.69.refs_5_
  31.9 2.3 %collective-permute-start.5 = (bf16[64,4096]{1,0:T(8,128)(2,1)S(1)}, bf16[64,4096]{1,0:T(8,128)(2,1)S(1)}, u32[]{:S(2)}, u32[]{:S(2)}) collective-permute-start(bf16[64,4096]{1,0:T(8,128)(2,1)S(1)} %shard_map.69.refs_5_), channel_id=1, source_target_pairs={{1,2},{2,1},{5,6},{6,5},{9,10},{10,9},{13,14},{14,13},{17,18},{18,... | collective-permute-start | bytes 1572872 | tf_op jit(solution)/shard_map/ppermute | solution.py:468
  34.2 1.5 %collective-permute-start.7 = (bf16[64,4096]{1,0:T(8,128)(2,1)S(1)}, bf16[64,4096]{1,0:T(8,128)(2,1)S(1)}, u32[]{:S(2)}, u32[]{:S(2)}) collective-permute-start(bf16[64,4096]{1,0:T(8,128)(2,1)S(1)} %get-tuple-element.34.refs_3_), channel_id=1, source_target_pairs={{0,1},{3,2},{4,5},{7,6},{8,9},{11,10},{12,13},{15,14},{16,17},{19,... | collective-permute-start | bytes 1572872 | tf_op jit(solution)/shard_map/ppermute | solution.py:468
  35.8 7.3 %collective-permute-done.4.refs_7_.right = bf16[64,4096]{1,0:T(8,128)(2,1)S(1)} collective-permute-done((bf16[64,4096]{1,0:T(8,128)(2,1)S(1)}, bf16[64,4096]{1,0:T(8,128)(2,1)S(1)}, u32[]{:S(2)}, u32[]{:S(2)}) %collective-permute-start.4) | collective-permute-done | bytes 524320 | tf_op jit(solution)/shard_map/ppermute | solution.py:468
  43.0 0.0 collective-permute-done.3.refs_6_.refs_4_
  43.1 5.5 %shard_map.70 = (bf16[64,4096]{1,0:T(8,128)(2,1)S(1)}, bf16[64,4096]{1,0:T(8,128)(2,1)S(1)}) custom-call(s32[8]{0:T(128)S(1)} %copy-done, bf16[2,256,1024]{2,1,0:T(8,128)(2,1)S(1)} %get-tuple-element.24.refs_1_, bf16[2,2,256,256]{3,2,1,0:T(8,128)(2,1)S(1)} %get-tuple-element.25.refs_2_, bf16[2,1536,256]{2,1,0:T(8,128)(2,1)S(1)} %get-tuple-element.26.refs_3_, ...), custom_call_target="tpu_custom_call" | custom-call | flops 1000 | bytes 1000 | tf_op jit(solution)/shard_map/pallas_call | solution.py:356
  48.6 0.0 collective-permute-done.5.refs_5_
  48.6 0.3 shard_map.71.rest_0_
  48.9 0.1 collective-permute-start.9
  48.9 0.1 shard_map.72
  49.1 0.2 collective-permute-start.6
  49.2 5.1 %collective-permute-done.7.right = bf16[64,4096]{1,0:T(8,128)(2,1)S(1)} collective-permute-done((bf16[64,4096]{1,0:T(8,128)(2,1)S(1)}, bf16[64,4096]{1,0:T(8,128)(2,1)S(1)}, u32[]{:S(2)}, u32[]{:S(2)}) %collective-permute-start.7) | collective-permute-done | bytes 524320 | tf_op jit(solution)/shard_map/ppermute | solution.py:468
  54.3 0.0 collective-permute-done.1.rest_1_.block
  54.3 0.1 shard_map.73
  54.4 0.1 collective-permute-start.8
  54.5 10.6 %collective-permute-done.6.refs_0_ = bf16[64,4096]{1,0:T(8,128)(2,1)S(1)} collective-permute-done((bf16[64,4096]{1,0:T(8,128)(2,1)S(1)}, bf16[64,4096]{1,0:T(8,128)(2,1)S(1)}, u32[]{:S(2)}, u32[]{:S(2)}) %collective-permute-start.6) | collective-permute-done | bytes 524320 | tf_op jit(solution)/shard_map/ppermute | solution.py:468
  65.1 11.1 %collective-permute-done.8.refs_1_ = bf16[64,4096]{1,0:T(8,128)(2,1)S(1)} collective-permute-done((bf16[64,4096]{1,0:T(8,128)(2,1)S(1)}, bf16[64,4096]{1,0:T(8,128)(2,1)S(1)}, u32[]{:S(2)}, u32[]{:S(2)}) %collective-permute-start.8) | collective-permute-done | bytes 524320 | tf_op jit(solution)/shard_map/ppermute | solution.py:468
  76.2 0.2 shard_map.74.wide
  76.4 1.2 %collective-permute-done.9.block = bf16[2,64,4096]{2,1,0:T(8,128)(2,1)S(1)} collective-permute-done((bf16[2,64,4096]{2,1,0:T(8,128)(2,1)S(1)}, bf16[2,64,4096]{2,1,0:T(8,128)(2,1)S(1)}, u32[]{:S(2)}, u32[]{:S(2)}) %collective-permute-start.9) | collective-permute-done | bytes 1048608 | tf_op jit(solution)/shard_map/ppermute | solution.py:468
  77.5 1.3 %shard_map.75 = bf16[64,2,4096]{2,1,0:T(2,128)(2,1)} custom-call(f32[2,64,4096]{2,1,0:T(8,128)S(1)} %shard_map.74.wide, bf16[2,64,4096]{2,1,0:T(8,128)(2,1)S(1)} %collective-permute-done.9.block), custom_call_target="tpu_custom_call" | custom-call | flops 1000 | bytes 1000 | tf_op jit(solution)/shard_map/pallas_call | solution.py:436
  (2 shorter events, 0.0 us)
Async XLA Ops:
  0.0 1.4 %copy-start = (s32[8]{0:T(128)S(1)}, s32[8]{0:T(128)}, u32[]{:S(2)}) copy-start(s32[8]{0:T(128)} %refs_0_.5) | copy-start | bytes 100
  0.1 20.5 %collective-permute-start = (bf16[64,4096]{1,0:T(8,128)(2,1)S(1)}, bf16[64,4096]{1,0:T(8,128)(2,1)S(1)}, u32[]{:S(2)}, u32[]{:S(2)}) collective-permute-start(bf16[64,4096]{1,0:T(8,128)(2,1)S(1)} %get-tuple-element.23.dep), channel_id=1, source_target_pairs={{0,1},{3,2},{4,5},{7,6},{8,9},{11,10},{12,13},{15,14},{16,17},{19,... | collective-permute-start | bytes 1572872 | tf_op jit(solution)/shard_map/ppermute | solution.py:468
  11.3 20.5 %collective-permute-start.2 = (bf16[64,4096]{1,0:T(8,128)(2,1)S(1)}, bf16[64,4096]{1,0:T(8,128)(2,1)S(1)}, u32[]{:S(2)}, u32[]{:S(2)}) collective-permute-start(bf16[64,4096]{1,0:T(8,128)(2,1)S(1)} %get-tuple-element.30.refs_5_.left), channel_id=1, source_target_pairs={{0,1},{3,2},{4,5},{7,6},{8,9},{11,10},{12,13},{15,14},{16,17},{19,... | collective-permute-start | bytes 1572872 | tf_op jit(solution)/shard_map/ppermute | solution.py:468
  18.4 24.7 %collective-permute-start.4 = (bf16[64,4096]{1,0:T(8,128)(2,1)S(1)}, bf16[64,4096]{1,0:T(8,128)(2,1)S(1)}, u32[]{:S(2)}, u32[]{:S(2)}) collective-permute-start(bf16[64,4096]{1,0:T(8,128)(2,1)S(1)} %get-tuple-element.31.rest_0_.refs_2_), channel_id=1, source_target_pairs={{0,1},{3,2},{4,5},{7,6},{8,9},{11,10},{12,13},{15,14},{16,17},{19,... | collective-permute-start | bytes 1572872 | tf_op jit(solution)/shard_map/ppermute | solution.py:468
  20.7 22.3 %collective-permute-start.3 = (bf16[64,4096]{1,0:T(8,128)(2,1)S(1)}, bf16[64,4096]{1,0:T(8,128)(2,1)S(1)}, u32[]{:S(2)}, u32[]{:S(2)}) collective-permute-start(bf16[64,4096]{1,0:T(8,128)(2,1)S(1)} %shard_map.67.refs_6_), channel_id=1, source_target_pairs={{1,2},{2,1},{5,6},{6,5},{9,10},{10,9},{13,14},{14,13},{17,18},{18,... | collective-permute-start | bytes 1572872 | tf_op jit(solution)/shard_map/ppermute | solution.py:468
  28.2 26.1 %collective-permute-start.1 = (bf16[2,64,4096]{2,1,0:T(8,128)(2,1)S(1)}, bf16[2,64,4096]{2,1,0:T(8,128)(2,1)S(1)}, u32[]{:S(2)}, u32[]{:S(2)}) collective-permute-start(bf16[2,64,4096]{2,1,0:T(8,128)(2,1)S(1)} %shard_map.68.rest_0_.plain), channel_id=1, source_target_pairs={{1,5},{2,6},{5,9},{6,10},{9,13},{10,14},{13,17},{14,18},{17,21},{1... | collective-permute-start | bytes 3145736 | tf_op jit(solution)/shard_map/ppermute | solution.py:468
  31.9 16.7 %collective-permute-start.5 = (bf16[64,4096]{1,0:T(8,128)(2,1)S(1)}, bf16[64,4096]{1,0:T(8,128)(2,1)S(1)}, u32[]{:S(2)}, u32[]{:S(2)}) collective-permute-start(bf16[64,4096]{1,0:T(8,128)(2,1)S(1)} %shard_map.69.refs_5_), channel_id=1, source_target_pairs={{1,2},{2,1},{5,6},{6,5},{9,10},{10,9},{13,14},{14,13},{17,18},{18,... | collective-permute-start | bytes 1572872 | tf_op jit(solution)/shard_map/ppermute | solution.py:468
  34.2 20.1 %collective-permute-start.7 = (bf16[64,4096]{1,0:T(8,128)(2,1)S(1)}, bf16[64,4096]{1,0:T(8,128)(2,1)S(1)}, u32[]{:S(2)}, u32[]{:S(2)}) collective-permute-start(bf16[64,4096]{1,0:T(8,128)(2,1)S(1)} %get-tuple-element.34.refs_3_), channel_id=1, source_target_pairs={{0,1},{3,2},{4,5},{7,6},{8,9},{11,10},{12,13},{15,14},{16,17},{19,... | collective-permute-start | bytes 1572872 | tf_op jit(solution)/shard_map/ppermute | solution.py:468
  48.9 28.7 %collective-permute-start.9 = (bf16[2,64,4096]{2,1,0:T(8,128)(2,1)S(1)}, bf16[2,64,4096]{2,1,0:T(8,128)(2,1)S(1)}, u32[]{:S(2)}, u32[]{:S(2)}) collective-permute-start(bf16[2,64,4096]{2,1,0:T(8,128)(2,1)S(1)} %shard_map.71.rest_0_), channel_id=1, source_target_pairs={{0,5},{3,6},{1,4},{2,7},{4,9},{7,10},{5,8},{6,11},{8,13},{11,14},{... | collective-permute-start | bytes 3145736 | tf_op jit(solution)/shard_map/ppermute | solution.py:468
  49.1 16.0 %collective-permute-start.6 = (bf16[64,4096]{1,0:T(8,128)(2,1)S(1)}, bf16[64,4096]{1,0:T(8,128)(2,1)S(1)}, u32[]{:S(2)}, u32[]{:S(2)}) collective-permute-start(bf16[64,4096]{1,0:T(8,128)(2,1)S(1)} %shard_map.72), channel_id=1, source_target_pairs={{1,6},{2,5},{0,4},{3,7},{5,10},{6,9},{4,8},{7,11},{9,14},{10,13},{... | collective-permute-start | bytes 1572872 | tf_op jit(solution)/shard_map/ppermute | solution.py:468
  54.4 21.7 %collective-permute-start.8 = (bf16[64,4096]{1,0:T(8,128)(2,1)S(1)}, bf16[64,4096]{1,0:T(8,128)(2,1)S(1)}, u32[]{:S(2)}, u32[]{:S(2)}) collective-permute-start(bf16[64,4096]{1,0:T(8,128)(2,1)S(1)} %shard_map.73), channel_id=1, source_target_pairs={{1,6},{2,5},{0,4},{3,7},{5,10},{6,9},{4,8},{7,11},{9,14},{10,13},{... | collective-permute-start | bytes 1572872 | tf_op jit(solution)/shard_map/ppermute | solution.py:468

commit v5 on v4

--- a/solution.py
+++ b/solution.py
@@ -96,11 +96,14 @@
             out[:, here] = product[index * rows : (index + 1) * rows].astype(out.dtype)
 
 
+def weight_parts(columns):
+    most = columns * 3 // 4
+    return [pl.ds(0, most), pl.ds(most, columns - most)]
+
+
 def project_arriving(heads_ref, w_ref, outs, copies):
-    part_columns = w_ref.shape[1] // len(copies)
-    for part, copy in enumerate(copies):
+    for here, copy in zip(weight_parts(w_ref.shape[1]), copies):
         copy.wait()
-        here = pl.ds(part * part_columns, part_columns)
         project(heads_ref, w_ref.at[:, here], [out.at[:, here] for out in outs])
 
 
@@ -115,9 +118,7 @@
             pairs.append((new_kv.at[tick, part, :, lanes], fresh_ref.at[tick, part]))
     for part in range(2):
         pairs.append((cache_kv.at[part, :, lanes], cache_ref.at[part]))
-    part_columns = w_ref.shape[1] // WEIGHT_PARTS
-    for part in range(WEIGHT_PARTS):
-        here = pl.ds(part * part_columns, part_columns)
+    for here in weight_parts(w_ref.shape[1]):
         pairs.append((out_weight.at[0, :, here], w_ref.at[:, here]))
     copies = [
         pltpu.make_async_copy(source, target, sem.at[index])

time: 79.3 us -> 79.5 us (level)
  no operation moved by 1% of the time
where the time goes in v5:
time: 79.5 us; the launch traced here: 79.3 us
  waiting for transfers between devices  38 us (48%)
  Pallas kernels  29 us (36%)
  starting transfers between devices  12 us (15%)
    ppermute x10, waiting for transfers between devices, send(): return lax.ppermute(block, ('section', 'head'), route)  38 us
    pallas_call x3, Pallas kernels, project_rows(): pl.pallas_call(functools.partial(rows_kernel, ticks, rows, choose, names)...  16.7 us
    ppermute x10, starting transfers between devices, send(): return lax.ppermute(block, ('section', 'head'), route)  12 us
    pallas_call x1, Pallas kernels, second_rows(): pl.pallas_call(functools.partial(second_kernel, ticks, rows, choose, acti...  9.92 us
  transfers between devices with their start and end apart: 10, of which 7 were waited for; matrix products, arithmetic and copies ran while one was open for 0% of the time, Pallas kernels for 35%

profile of v5, /device:TPU:16, one launch (start us, length us, event | category | flops | bytes accessed | tf_op | source)
XLA Modules:
  0.0 79.3 jit_solution(11457677019973344794)
XLA Ops:
  0.0 0.1 shard_map.64
  0.1 1.3 %collective-permute-start = (bf16[64,4096]{1,0:T(8,128)(2,1)S(1)}, bf16[64,4096]{1,0:T(8,128)(2,1)S(1)}, u32[]{:S(2)}, u32[]{:S(2)}) collective-permute-start(bf16[64,4096]{1,0:T(8,128)(2,1)S(1)} %get-tuple-element.23.dep), channel_id=1, source_target_pairs={{0,1},{3,2},{4,5},{7,6},{8,9},{11,10},{12,13},{15,14},{16,17},{19,... | collective-permute-start | bytes 1572872 | tf_op jit(solution)/shard_map/ppermute | solution.py:469
  1.4 9.9 %shard_map.65 = (bf16[64,4096]{1,0:T(8,128)(2,1)S(1)}, bf16[64,4096]{1,0:T(8,128)(2,1)S(1)}, bf16[2,256,1024]{2,1,0:T(8,128)(2,1)S(1)}, bf16[2,64,4096]{2,1,0:T(...) custom-call(s32[8]{0:T(128)S(1)} %copy-done, ...), custom_call_target="tpu_custom_call", output_to_operand_aliasing={{4}: (6, {}), {5}: (7, {}), {6}: (8, {})} | custom-call | flops 1000 | bytes 1000 | tf_op jit(solution)/shard_map/pallas_call | solution.py:319
  11.3 1.5 %collective-permute-start.2 = (bf16[64,4096]{1,0:T(8,128)(2,1)S(1)}, bf16[64,4096]{1,0:T(8,128)(2,1)S(1)}, u32[]{:S(2)}, u32[]{:S(2)}) collective-permute-start(bf16[64,4096]{1,0:T(8,128)(2,1)S(1)} %get-tuple-element.30.refs_5_.left), channel_id=1, source_target_pairs={{0,1},{3,2},{4,5},{7,6},{8,9},{11,10},{12,13},{15,14},{16,17},{19,... | collective-permute-start | bytes 1572872 | tf_op jit(solution)/shard_map/ppermute | solution.py:469
  12.8 5.5 %shard_map.66 = (bf16[64,4096]{1,0:T(8,128)(2,1)S(1)}, bf16[64,4096]{1,0:T(8,128)(2,1)S(1)}) custom-call(s32[8]{0:T(128)S(1)} %copy-done, bf16[2,256,1024]{2,1,0:T(8,128)(2,1)S(1)} %get-tuple-element.24.refs_1_, bf16[2,2,256,256]{3,2,1,0:T(8,128)(2,1)S(1)} %get-tuple-element.25.refs_2_, bf16[2,1536,256]{2,1,0:T(8,128)(2,1)S(1)} %get-tuple-element.26.refs_3_, ...), custom_call_target="tpu_custom_call" | custom-call | flops 1000 | bytes 1000 | tf_op jit(solution)/shard_map/pallas_call | solution.py:357
  18.4 1.3 %collective-permute-start.4 = (bf16[64,4096]{1,0:T(8,128)(2,1)S(1)}, bf16[64,4096]{1,0:T(8,128)(2,1)S(1)}, u32[]{:S(2)}, u32[]{:S(2)}) collective-permute-start(bf16[64,4096]{1,0:T(8,128)(2,1)S(1)} %get-tuple-element.31.rest_0_.refs_2_), channel_id=1, source_target_pairs={{0,1},{3,2},{4,5},{7,6},{8,9},{11,10},{12,13},{15,14},{16,17},{19,... | collective-permute-start | bytes 1572872 | tf_op jit(solution)/shard_map/ppermute | solution.py:469
  19.7 1.2 %collective-permute-done.right = bf16[64,4096]{1,0:T(8,128)(2,1)S(1)} collective-permute-done((bf16[64,4096]{1,0:T(8,128)(2,1)S(1)}, bf16[64,4096]{1,0:T(8,128)(2,1)S(1)}, u32[]{:S(2)}, u32[]{:S(2)}) %collective-permute-start) | collective-permute-done | bytes 524320 | tf_op jit(solution)/shard_map/ppermute | solution.py:469
  20.8 0.1 shard_map.67.refs_6_
  20.9 1.9 %collective-permute-start.3 = (bf16[64,4096]{1,0:T(8,128)(2,1)S(1)}, bf16[64,4096]{1,0:T(8,128)(2,1)S(1)}, u32[]{:S(2)}, u32[]{:S(2)}) collective-permute-start(bf16[64,4096]{1,0:T(8,128)(2,1)S(1)} %shard_map.67.refs_6_), channel_id=1, source_target_pairs={{1,2},{2,1},{5,6},{6,5},{9,10},{10,9},{13,14},{14,13},{17,18},{18,... | collective-permute-start | bytes 1572872 | tf_op jit(solution)/shard_map/ppermute | solution.py:469
  22.9 5.6 %shard_map.68.rest_0_.plain = bf16[2,64,4096]{2,1,0:T(8,128)(2,1)S(1)} custom-call(s32[8]{0:T(128)S(1)} %copy-done, bf16[2,256,1024]{2,1,0:T(8,128)(2,1)S(1)} %get-tuple-element.24.refs_1_, bf16[2,2,256,256]{3,2,1,0:T(8,128)(2,1)S(1)} %get-tuple-element.25.refs_2_, bf16[2,1536,256]{2,1,0:T(8,128)(2,1)S(1)} %get-tuple-element.26.refs_3_, ...), custom_call_target="tpu_custom_call" | custom-call | flops 4499999744 | bytes 1000 | tf_op jit(solution)/shard_map/pallas_call | solution.py:357
  28.5 1.9 %collective-permute-start.1 = (bf16[2,64,4096]{2,1,0:T(8,128)(2,1)S(1)}, bf16[2,64,4096]{2,1,0:T(8,128)(2,1)S(1)}, u32[]{:S(2)}, u32[]{:S(2)}) collective-permute-start(bf16[2,64,4096]{2,1,0:T(8,128)(2,1)S(1)} %shard_map.68.rest_0_.plain), channel_id=1, source_target_pairs={{1,5},{2,6},{5,9},{6,10},{9,13},{10,14},{13,17},{14,18},{17,21},{1... | collective-permute-start | bytes 3145736 | tf_op jit(solution)/shard_map/ppermute | solution.py:469
  30.4 1.7 %collective-permute-done.2.right = bf16[64,4096]{1,0:T(8,128)(2,1)S(1)} collective-permute-done((bf16[64,4096]{1,0:T(8,128)(2,1)S(1)}, bf16[64,4096]{1,0:T(8,128)(2,1)S(1)}, u32[]{:S(2)}, u32[]{:S(2)}) %collective-permute-start.2) | collective-permute-done | bytes 524320 | tf_op jit(solution)/shard_map/ppermute | solution.py:469
  32.0 0.1 shard_map.69.refs_5_
  32.2 2.3 %collective-permute-start.5 = (bf16[64,4096]{1,0:T(8,128)(2,1)S(1)}, bf16[64,4096]{1,0:T(8,128)(2,1)S(1)}, u32[]{:S(2)}, u32[]{:S(2)}) collective-permute-start(bf16[64,4096]{1,0:T(8,128)(2,1)S(1)} %shard_map.69.refs_5_), channel_id=1, source_target_pairs={{1,2},{2,1},{5,6},{6,5},{9,10},{10,9},{13,14},{14,13},{17,18},{18,... | collective-permute-start | bytes 1572872 | tf_op jit(solution)/shard_map/ppermute | solution.py:469
  34.5 1.5 %collective-permute-start.7 = (bf16[64,4096]{1,0:T(8,128)(2,1)S(1)}, bf16[64,4096]{1,0:T(8,128)(2,1)S(1)}, u32[]{:S(2)}, u32[]{:S(2)}) collective-permute-start(bf16[64,4096]{1,0:T(8,128)(2,1)S(1)} %get-tuple-element.34.refs_3_), channel_id=1, source_target_pairs={{0,1},{3,2},{4,5},{7,6},{8,9},{11,10},{12,13},{15,14},{16,17},{19,... | collective-permute-start | bytes 1572872 | tf_op jit(solution)/shard_map/ppermute | solution.py:469
  36.0 7.3 %collective-permute-done.4.refs_7_.right = bf16[64,4096]{1,0:T(8,128)(2,1)S(1)} collective-permute-done((bf16[64,4096]{1,0:T(8,128)(2,1)S(1)}, bf16[64,4096]{1,0:T(8,128)(2,1)S(1)}, u32[]{:S(2)}, u32[]{:S(2)}) %collective-permute-start.4) | collective-permute-done | bytes 524320 | tf_op jit(solution)/shard_map/ppermute | solution.py:469
  43.3 0.0 collective-permute-done.3.refs_6_.refs_4_
  43.3 5.5 %shard_map.70 = (bf16[64,4096]{1,0:T(8,128)(2,1)S(1)}, bf16[64,4096]{1,0:T(8,128)(2,1)S(1)}) custom-call(s32[8]{0:T(128)S(1)} %copy-done, bf16[2,256,1024]{2,1,0:T(8,128)(2,1)S(1)} %get-tuple-element.24.refs_1_, bf16[2,2,256,256]{3,2,1,0:T(8,128)(2,1)S(1)} %get-tuple-element.25.refs_2_, bf16[2,1536,256]{2,1,0:T(8,128)(2,1)S(1)} %get-tuple-element.26.refs_3_, ...), custom_call_target="tpu_custom_call" | custom-call | flops 1000 | bytes 1000 | tf_op jit(solution)/shard_map/pallas_call | solution.py:357
  48.8 0.0 collective-permute-done.5.refs_5_
  48.8 0.3 shard_map.71.rest_0_
  49.1 0.1 collective-permute-start.9
  49.2 0.1 shard_map.72
  49.3 0.2 collective-permute-start.6
  49.5 5.1 %collective-permute-done.7.right = bf16[64,4096]{1,0:T(8,128)(2,1)S(1)} collective-permute-done((bf16[64,4096]{1,0:T(8,128)(2,1)S(1)}, bf16[64,4096]{1,0:T(8,128)(2,1)S(1)}, u32[]{:S(2)}, u32[]{:S(2)}) %collective-permute-start.7) | collective-permute-done | bytes 524320 | tf_op jit(solution)/shard_map/ppermute | solution.py:469
  54.5 0.0 collective-permute-done.1.rest_1_.block
  54.5 0.1 shard_map.73
  54.6 0.1 collective-permute-start.8
  54.7 10.6 %collective-permute-done.6.refs_0_ = bf16[64,4096]{1,0:T(8,128)(2,1)S(1)} collective-permute-done((bf16[64,4096]{1,0:T(8,128)(2,1)S(1)}, bf16[64,4096]{1,0:T(8,128)(2,1)S(1)}, u32[]{:S(2)}, u32[]{:S(2)}) %collective-permute-start.6) | collective-permute-done | bytes 524320 | tf_op jit(solution)/shard_map/ppermute | solution.py:469
  65.3 11.1 %collective-permute-done.8.refs_1_ = bf16[64,4096]{1,0:T(8,128)(2,1)S(1)} collective-permute-done((bf16[64,4096]{1,0:T(8,128)(2,1)S(1)}, bf16[64,4096]{1,0:T(8,128)(2,1)S(1)}, u32[]{:S(2)}, u32[]{:S(2)}) %collective-permute-start.8) | collective-permute-done | bytes 524320 | tf_op jit(solution)/shard_map/ppermute | solution.py:469
  76.4 0.2 shard_map.74.wide
  76.6 1.2 %collective-permute-done.9.block = bf16[2,64,4096]{2,1,0:T(8,128)(2,1)S(1)} collective-permute-done((bf16[2,64,4096]{2,1,0:T(8,128)(2,1)S(1)}, bf16[2,64,4096]{2,1,0:T(8,128)(2,1)S(1)}, u32[]{:S(2)}, u32[]{:S(2)}) %collective-permute-start.9) | collective-permute-done | bytes 1048608 | tf_op jit(solution)/shard_map/ppermute | solution.py:469
  77.8 1.3 %shard_map.75 = bf16[64,2,4096]{2,1,0:T(2,128)(2,1)} custom-call(f32[2,64,4096]{2,1,0:T(8,128)S(1)} %shard_map.74.wide, bf16[2,64,4096]{2,1,0:T(8,128)(2,1)S(1)} %collective-permute-done.9.block), custom_call_target="tpu_custom_call" | custom-call | flops 1000 | bytes 1000 | tf_op jit(solution)/shard_map/pallas_call | solution.py:437
  (2 shorter events, 0.0 us)
Async XLA Ops:
  0.0 1.4 %copy-start = (s32[8]{0:T(128)S(1)}, s32[8]{0:T(128)}, u32[]{:S(2)}) copy-start(s32[8]{0:T(128)} %refs_0_.5) | copy-start | bytes 100
  0.1 20.7 %collective-permute-start = (bf16[64,4096]{1,0:T(8,128)(2,1)S(1)}, bf16[64,4096]{1,0:T(8,128)(2,1)S(1)}, u32[]{:S(2)}, u32[]{:S(2)}) collective-permute-start(bf16[64,4096]{1,0:T(8,128)(2,1)S(1)} %get-tuple-element.23.dep), channel_id=1, source_target_pairs={{0,1},{3,2},{4,5},{7,6},{8,9},{11,10},{12,13},{15,14},{16,17},{19,... | collective-permute-start | bytes 1572872 | tf_op jit(solution)/shard_map/ppermute | solution.py:469
  11.3 20.7 %collective-permute-start.2 = (bf16[64,4096]{1,0:T(8,128)(2,1)S(1)}, bf16[64,4096]{1,0:T(8,128)(2,1)S(1)}, u32[]{:S(2)}, u32[]{:S(2)}) collective-permute-start(bf16[64,4096]{1,0:T(8,128)(2,1)S(1)} %get-tuple-element.30.refs_5_.left), channel_id=1, source_target_pairs={{0,1},{3,2},{4,5},{7,6},{8,9},{11,10},{12,13},{15,14},{16,17},{19,... | collective-permute-start | bytes 1572872 | tf_op jit(solution)/shard_map/ppermute | solution.py:469
  18.4 24.9 %collective-permute-start.4 = (bf16[64,4096]{1,0:T(8,128)(2,1)S(1)}, bf16[64,4096]{1,0:T(8,128)(2,1)S(1)}, u32[]{:S(2)}, u32[]{:S(2)}) collective-permute-start(bf16[64,4096]{1,0:T(8,128)(2,1)S(1)} %get-tuple-element.31.rest_0_.refs_2_), channel_id=1, source_target_pairs={{0,1},{3,2},{4,5},{7,6},{8,9},{11,10},{12,13},{15,14},{16,17},{19,... | collective-permute-start | bytes 1572872 | tf_op jit(solution)/shard_map/ppermute | solution.py:469
  20.9 22.3 %collective-permute-start.3 = (bf16[64,4096]{1,0:T(8,128)(2,1)S(1)}, bf16[64,4096]{1,0:T(8,128)(2,1)S(1)}, u32[]{:S(2)}, u32[]{:S(2)}) collective-permute-start(bf16[64,4096]{1,0:T(8,128)(2,1)S(1)} %shard_map.67.refs_6_), channel_id=1, source_target_pairs={{1,2},{2,1},{5,6},{6,5},{9,10},{10,9},{13,14},{14,13},{17,18},{18,... | collective-permute-start | bytes 1572872 | tf_op jit(solution)/shard_map/ppermute | solution.py:469
  28.5 26.1 %collective-permute-start.1 = (bf16[2,64,4096]{2,1,0:T(8,128)(2,1)S(1)}, bf16[2,64,4096]{2,1,0:T(8,128)(2,1)S(1)}, u32[]{:S(2)}, u32[]{:S(2)}) collective-permute-start(bf16[2,64,4096]{2,1,0:T(8,128)(2,1)S(1)} %shard_map.68.rest_0_.plain), channel_id=1, source_target_pairs={{1,5},{2,6},{5,9},{6,10},{9,13},{10,14},{13,17},{14,18},{17,21},{1... | collective-permute-start | bytes 3145736 | tf_op jit(solution)/shard_map/ppermute | solution.py:469
  32.2 16.7 %collective-permute-start.5 = (bf16[64,4096]{1,0:T(8,128)(2,1)S(1)}, bf16[64,4096]{1,0:T(8,128)(2,1)S(1)}, u32[]{:S(2)}, u32[]{:S(2)}) collective-permute-start(bf16[64,4096]{1,0:T(8,128)(2,1)S(1)} %shard_map.69.refs_5_), channel_id=1, source_target_pairs={{1,2},{2,1},{5,6},{6,5},{9,10},{10,9},{13,14},{14,13},{17,18},{18,... | collective-permute-start | bytes 1572872 | tf_op jit(solution)/shard_map/ppermute | solution.py:469
  34.5 20.1 %collective-permute-start.7 = (bf16[64,4096]{1,0:T(8,128)(2,1)S(1)}, bf16[64,4096]{1,0:T(8,128)(2,1)S(1)}, u32[]{:S(2)}, u32[]{:S(2)}) collective-permute-start(bf16[64,4096]{1,0:T(8,128)(2,1)S(1)} %get-tuple-element.34.refs_3_), channel_id=1, source_target_pairs={{0,1},{3,2},{4,5},{7,6},{8,9},{11,10},{12,13},{15,14},{16,17},{19,... | collective-permute-start | bytes 1572872 | tf_op jit(solution)/shard_map/ppermute | solution.py:469
  49.1 28.7 %collective-permute-start.9 = (bf16[2,64,4096]{2,1,0:T(8,128)(2,1)S(1)}, bf16[2,64,4096]{2,1,0:T(8,128)(2,1)S(1)}, u32[]{:S(2)}, u32[]{:S(2)}) collective-permute-start(bf16[2,64,4096]{2,1,0:T(8,128)(2,1)S(1)} %shard_map.71.rest_0_), channel_id=1, source_target_pairs={{0,5},{3,6},{1,4},{2,7},{4,9},{7,10},{5,8},{6,11},{8,13},{11,14},{... | collective-permute-start | bytes 3145736 | tf_op jit(solution)/shard_map/ppermute | solution.py:469
  49.3 16.0 %collective-permute-start.6 = (bf16[64,4096]{1,0:T(8,128)(2,1)S(1)}, bf16[64,4096]{1,0:T(8,128)(2,1)S(1)}, u32[]{:S(2)}, u32[]{:S(2)}) collective-permute-start(bf16[64,4096]{1,0:T(8,128)(2,1)S(1)} %shard_map.72), channel_id=1, source_target_pairs={{1,6},{2,5},{0,4},{3,7},{5,10},{6,9},{4,8},{7,11},{9,14},{10,13},{... | collective-permute-start | bytes 1572872 | tf_op jit(solution)/shard_map/ppermute | solution.py:469
  54.6 21.7 %collective-permute-start.8 = (bf16[64,4096]{1,0:T(8,128)(2,1)S(1)}, bf16[64,4096]{1,0:T(8,128)(2,1)S(1)}, u32[]{:S(2)}, u32[]{:S(2)}) collective-permute-start(bf16[64,4096]{1,0:T(8,128)(2,1)S(1)} %shard_map.73), channel_id=1, source_target_pairs={{1,6},{2,5},{0,4},{3,7},{5,10},{6,9},{4,8},{7,11},{9,14},{10,13},{... | collective-permute-start | bytes 1572872 | tf_op jit(solution)/shard_map/ppermute | solution.py:469
